TPU v7x, 256 devices: a whole 4x4x8 slice. The times are simulated.
256 devices in a mesh: blk: 256 (over z, y, x, core).
Axes of the slice: x: 4, y: 4, z: 8, core: 2. Of those that a mesh axis runs over, the one named last changes fastest.
Arguments:
- images: bfloat16 [196608, 1152], P('blk'), may hold values from -0.15 to 0.15
- texts: bfloat16 [196608, 1152], P('blk'), may hold values from -0.15 to 0.15
- log_scale: float32 [1], replicated, may hold values from 3 to 4.1
- logit_bias: float32 [1], replicated, may hold values from -4 to -1
Outputs:
- row_loss: float32 [196608], P('blk')
- image_grad: float32 [196608, 1152], P('blk')
- text_grad: float32 [196608, 1152], P('blk')
All inputs are finite; a program needn't handle non-finite values.
Results may differ from a plain program's by a relative error of at most 0.0064.
Values may be sent and summed in bfloat16 or wider, within the bound.
No kernel may reach another device: no remote copies, remote signals or barrier semaphores. Data moves between devices by JAX's collectives and lax.ppermute only.
A program may use at most 64 MiB of HBM per device.

v0:
```python
import jax
import jax.numpy as jnp
from jax import lax
from jax.sharding import PartitionSpec as P

STEPS = 3


EPS = 1e-12


def passed_along(shard, axis, by):
    peers = lax.axis_size(axis)
    return lax.ppermute(shard, axis, [(i, (i + by) % peers) for i in range(peers)])


def normalize(raw):
    widened = raw.astype(jnp.float32)
    inverse = lax.rsqrt(jnp.sum(widened * widened, axis=1, keepdims=True) + EPS)
    return (widened * inverse, inverse)


def score_block(image_block, text_block, scale_now, shift_now, own):
    rows = image_block.shape[0]
    products = lax.dot_general(
        image_block, text_block, (((1,), (1,)), ((), ())), preferred_element_type=jnp.float32
    )
    logits = scale_now * products + shift_now
    if own:
        row_ids = lax.broadcasted_iota(jnp.int32, logits.shape, 0)
        col_ids = lax.broadcasted_iota(jnp.int32, logits.shape, 1)
        labels = jnp.where(row_ids == col_ids, 1.0, -1.0).astype(jnp.float32)
    else:
        labels = -jnp.ones_like(logits)
    losses = jax.nn.softplus(-labels * logits)
    slopes = (-labels * jax.nn.sigmoid(-labels * logits) / rows).astype(jnp.bfloat16)
    return (losses, slopes)


def back_norm(unit, inverse, grad_unit):
    return (grad_unit - unit * jnp.sum(unit * grad_unit, axis=1, keepdims=True)) * inverse


def per_device(images, texts, log_scale, logit_bias):
    scale_now = jnp.exp(log_scale[0])
    shift_now = logit_bias[0]
    rows = images.shape[0]
    image_unit, image_inverse = normalize(images)
    text_unit, text_inverse = normalize(texts)
    image_emb = image_unit.astype(jnp.bfloat16)
    own_text = text_unit.astype(jnp.bfloat16)
    current = own_text
    loss_sum = jnp.zeros((rows,), jnp.float32)
    image_acc = jnp.zeros(images.shape, jnp.float32)
    carried = jnp.zeros(images.shape, jnp.float32)
    for offset in range(STEPS):
        if offset > 0:
            current = passed_along(current, "blk", 1)
        losses, slopes = score_block(image_emb, current, scale_now, shift_now, offset == 0)
        loss_sum = loss_sum + jnp.sum(losses, axis=1)
        image_acc = image_acc + scale_now * jnp.dot(
            slopes, current, preferred_element_type=jnp.float32
        )
        partial_value = scale_now * lax.dot_general(
            slopes, image_emb, (((0,), (0,)), ((), ())), preferred_element_type=jnp.float32
        )
        if offset == 0:
            carried = partial_value
        else:
            carried = passed_along(carried, "blk", 1) + partial_value
    summed = passed_along(carried, "blk", -(STEPS - 1))
    row_loss = loss_sum / (STEPS * rows)
    image_grad = back_norm(image_unit, image_inverse, image_acc)
    text_grad = back_norm(text_unit, text_inverse, summed)
    return (row_loss, image_grad, text_grad)


def solution(mesh):
    placed = (P("blk", None), P("blk", None), P(), P())
    return jax.shard_map(
        per_device,
        mesh=mesh,
        in_specs=placed,
        out_specs=(P("blk"), P("blk", None), P("blk", None)),
        check_vma=False,
    )
```

profile of v0, /device:TPU:1, one launch (start us, length us, event | category | flops | bytes accessed | tf_op | source)
XLA Modules:
  0.0 232.9 jit_solution(11004330186000142625)
XLA Ops:
  2.1 2.0 fusion.15
  4.2 0.4 fusion.2
  4.5 0.4 fusion.11
  5.0 2.9 %fusion.16 = (f32[768]{0:T(1024)S(1)}, f32[768,768]{0,1:T(8,128)S(1)}) fusion(f32[]{:T(128)} %bitcast.8, bf16[768,1152]{1,0:T(8,128)(2,1)S(1)} %fusion.2, bf16[768,1152]{1,0:T(8,128)(2,1)S(1)} %copy-done.1, f32[768]{0:T(1024)S(1)} %add_rsqrt_fusion.1, f32[]{:T(128)} %bitcast), kind=kOutput, calls=%fused_computation.28 | convolution fusion | flops 1369275648 | bytes 5904392 | tf_op jit(solution)/shard_map/dot_general | solution.py:25
  7.8 2.2 convolution_multiply_fusion.2
  10.0 2.7 %collective-permute-start.2 = (f32[768,1152]{1,0:T(8,128)S(1)}, f32[768,1152]{1,0:T(8,128)S(1)}, u32[]{:S(2)}, u32[]{:S(2)}) collective-permute-start(f32[768,1152]{1,0:T(8,128)S(1)} %convolution_multiply_fusion.2), channel_id=1, source_target_pairs={{0,1},{1,2},{2,3},{3,4},{4,5},{5,6},{6,7},{7,8},{8,9},{9,10},{10,1... | collective-permute-start | bytes 10616840 | tf_op jit(solution)/shard_map/ppermute | solution.py:14
  12.7 0.1 collective-permute-start
  12.8 57.3 %collective-permute-done = bf16[768,1152]{1,0:T(8,128)(2,1)S(1)} collective-permute-done((bf16[768,1152]{1,0:T(8,128)(2,1)S(1)}, bf16[768,1152]{1,0:T(8,128)(2,1)S(1)}, u32[]{:S(2)}, u32[]{:S(2)}) %collective-permute-start) | collective-permute-done | bytes 1769504 | tf_op jit(solution)/shard_map/ppermute | solution.py:14
  70.1 2.8 %fusion.17 = (f32[768]{0:T(1024)S(1)}, f32[768,768]{0,1:T(8,128)S(1)}) fusion(f32[]{:T(128)} %bitcast.10, f32[]{:T(128)} %bitcast, bf16[768,1152]{1,0:T(8,128)(2,1)S(1)} %collective-permute-done, bf16[768,1152]{1,0:T(8,128)(2,1)S(1)} %copy-done.1, f32[768]{0:T(1024)S(1)} %add_rsqrt_fusion.1), kind=kOutput, calls=%fused_computation.29 | convolution fusion | flops 1366916352 | bytes 5904392 | tf_op jit(solution)/shard_map/dot_general | solution.py:25
  72.9 2.2 fusion.6
  75.2 2.7 %collective-permute-start.3 = (f32[768,1152]{1,0:T(8,128)S(1)}, f32[768,1152]{1,0:T(8,128)S(1)}, u32[]{:S(2)}, u32[]{:S(2)}) collective-permute-start(f32[768,1152]{1,0:T(8,128)S(1)} %fusion.6), channel_id=1, source_target_pairs={{0,1},{1,2},{2,3},{3,4},{4,5},{5,6},{6,7},{7,8},{8,9},{9,10},{10,1... | collective-permute-start | bytes 10616840 | tf_op jit(solution)/shard_map/ppermute | solution.py:14
  78.0 57.3 %collective-permute-done.1 = bf16[768,1152]{1,0:T(8,128)(2,1)S(1)} collective-permute-done((bf16[768,1152]{1,0:T(8,128)(2,1)S(1)}, bf16[768,1152]{1,0:T(8,128)(2,1)S(1)}, u32[]{:S(2)}, u32[]{:S(2)}) %collective-permute-start.1) | collective-permute-done | bytes 1769504 | tf_op jit(solution)/shard_map/ppermute | solution.py:14
  135.3 2.8 %fusion.18 = (f32[768]{0:T(1024)S(1)}, f32[768,768]{0,1:T(8,128)S(1)}) fusion(f32[]{:T(128)} %bitcast.9, f32[]{:T(128)} %bitcast, bf16[768,1152]{1,0:T(8,128)(2,1)S(1)} %collective-permute-done.1, bf16[768,1152]{1,0:T(8,128)(2,1)S(1)} %copy-done.1, f32[768]{0:T(1024)S(1)} %add_rsqrt_fusion.1), kind=kOutput, calls=%fused_computation.30 | convolution fusion | flops 1366916352 | bytes 5904392 | tf_op jit(solution)/shard_map/dot_general | solution.py:25
  138.1 2.2 convolution_multiply_fusion
  140.3 0.4 add.84
  140.7 14.2 %collective-permute-start.4 = (f32[768,1152]{1,0:T(8,128)S(1)}, f32[768,1152]{1,0:T(8,128)S(1)}, u32[]{:S(2)}, u32[]{:S(2)}) collective-permute-start(f32[768,1152]{1,0:T(8,128)S(1)} %add.84), channel_id=1, source_target_pairs={{0,254},{1,255},{2,0},{3,1},{4,2},{5,3},{6,4},{7,5},{8,6},{9,7},{1... | collective-permute-start | bytes 10616840 | tf_op jit(solution)/shard_map/ppermute | solution.py:14
  154.9 1.8 fusion.19
  156.7 1.9 convolution_add_fusion.1
  158.6 0.6 add_multiply_fusion.1
  159.2 2.5 %fusion.8 = (f32[768]{0:T(1024)S(1)}, f32[768,1152]{1,0:T(8,128)S(1)}) fusion(bf16[768,1152]{1,0:T(8,128)(2,1)S(1)} %copy-done.1, f32[768]{0:T(1024)S(1)} %add_rsqrt_fusion.1, f32[]{:T(128)} %bitcast, f32[768,1152]{1,0:T(8,128)S(1)} %convolution_add_fusion.1, bf16[768,1152]{1,0:T(8,128)(2,1)S(1)} %collective-permute-done.1, ...), kind=kOutput, calls=%fused_computation.20 | convolution fusion | flops 1368390912 | bytes 12982280 | tf_op jit(solution)/shard_map/dot_general | solution.py:61
  161.8 2.5 %fusion.10 = f32[768,1152]{1,0:T(8,128)} fusion(f32[768,1152]{1,0:T(8,128)S(1)} %get-tuple-element.10, bf16[768,1152]{1,0:T(8,128)(2,1)S(1)} %copy-done.1, f32[768]{0:T(1024)S(1)} %get-tuple-element.9, f32[768]{0:T(1024)S(1)} %add_rsqrt_fusion.1), kind=kLoop, calls=%fused_computation.22 | loop fusion | flops 4423680 | bytes 8853504 | tf_op jit(solution)/shard_map/mul | solution.py:41
  164.2 65.6 %collective-permute-done.4 = f32[768,1152]{1,0:T(8,128)S(1)} collective-permute-done((f32[768,1152]{1,0:T(8,128)S(1)}, f32[768,1152]{1,0:T(8,128)S(1)}, u32[]{:S(2)}, u32[]{:S(2)}) %collective-permute-start.4) | collective-permute-done | bytes 3538976 | tf_op jit(solution)/shard_map/ppermute | solution.py:14
  229.9 0.6 fusion.12
  230.5 2.5 %fusion.14 = f32[768,1152]{1,0:T(8,128)} fusion(f32[768,1152]{1,0:T(8,128)S(1)} %collective-permute-done.4, bf16[768,1152]{1,0:T(8,128)(2,1)S(1)} %copy-done, f32[768]{0:T(1024)S(1)} %fusion.12, f32[768]{0:T(1024)S(1)} %add_rsqrt_fusion), kind=kLoop, calls=%fused_computation.26 | loop fusion | flops 4423680 | bytes 8853504 | tf_op jit(solution)/shard_map/mul | solution.py:41
  (9 shorter events, 0.1 us)
Async XLA Ops:
  0.6 3.5 %copy-start = (bf16[768,1152]{1,0:T(8,128)(2,1)S(1)}, bf16[768,1152]{1,0:T(8,128)(2,1)}, u32[]{:S(2)}) copy-start(bf16[768,1152]{1,0:T(8,128)(2,1)} %param.5) | copy-start | bytes 5308420
  2.1 2.4 %copy-start.1 = (bf16[768,1152]{1,0:T(8,128)(2,1)S(1)}, bf16[768,1152]{1,0:T(8,128)(2,1)}, u32[]{:S(2)}) copy-start(bf16[768,1152]{1,0:T(8,128)(2,1)} %param.4) | copy-start | bytes 5308420
  10.0 62.9 %collective-permute-start.2 = (f32[768,1152]{1,0:T(8,128)S(1)}, f32[768,1152]{1,0:T(8,128)S(1)}, u32[]{:S(2)}, u32[]{:S(2)}) collective-permute-start(f32[768,1152]{1,0:T(8,128)S(1)} %convolution_multiply_fusion.2), channel_id=1, source_target_pairs={{0,1},{1,2},{2,3},{3,4},{4,5},{5,6},{6,7},{7,8},{8,9},{9,10},{10,1... | collective-permute-start | bytes 10616840 | tf_op jit(solution)/shard_map/ppermute | solution.py:14
  12.7 57.4 %collective-permute-start = (bf16[768,1152]{1,0:T(8,128)(2,1)S(1)}, bf16[768,1152]{1,0:T(8,128)(2,1)S(1)}, u32[]{:S(2)}, u32[]{:S(2)}) collective-permute-start(bf16[768,1152]{1,0:T(8,128)(2,1)S(1)} %fusion.2), channel_id=1, source_target_pairs={{0,1},{1,2},{2,3},{3,4},{4,5},{5,6},{6,7},{7,8},{8,9},{9,10},{10,1... | collective-permute-start | bytes 5308424 | tf_op jit(solution)/shard_map/ppermute | solution.py:14
  75.2 65.1 %collective-permute-start.3 = (f32[768,1152]{1,0:T(8,128)S(1)}, f32[768,1152]{1,0:T(8,128)S(1)}, u32[]{:S(2)}, u32[]{:S(2)}) collective-permute-start(f32[768,1152]{1,0:T(8,128)S(1)} %fusion.6), channel_id=1, source_target_pairs={{0,1},{1,2},{2,3},{3,4},{4,5},{5,6},{6,7},{7,8},{8,9},{9,10},{10,1... | collective-permute-start | bytes 10616840 | tf_op jit(solution)/shard_map/ppermute | solution.py:14
  77.9 57.4 %collective-permute-start.1 = (bf16[768,1152]{1,0:T(8,128)(2,1)S(1)}, bf16[768,1152]{1,0:T(8,128)(2,1)S(1)}, u32[]{:S(2)}, u32[]{:S(2)}) collective-permute-start(bf16[768,1152]{1,0:T(8,128)(2,1)S(1)} %collective-permute-done), channel_id=1, source_target_pairs={{0,1},{1,2},{2,3},{3,4},{4,5},{5,6},{6,7},{7,8},{8,9},{9,10},{10,1... | collective-permute-start | bytes 5308424 | tf_op jit(solution)/shard_map/ppermute | solution.py:14
  140.7 89.2 %collective-permute-start.4 = (f32[768,1152]{1,0:T(8,128)S(1)}, f32[768,1152]{1,0:T(8,128)S(1)}, u32[]{:S(2)}, u32[]{:S(2)}) collective-permute-start(f32[768,1152]{1,0:T(8,128)S(1)} %add.84), channel_id=1, source_target_pairs={{0,254},{1,255},{2,0},{3,1},{4,2},{5,3},{6,4},{7,5},{8,6},{9,7},{1... | collective-permute-start | bytes 10616840 | tf_op jit(solution)/shard_map/ppermute | solution.py:14
where the time goes:
time: 234 us; the launch traced here: 233 us
  waiting for transfers between devices  180 us (77%)
  matrix products  21.4 us (9%)
  starting transfers between devices  19.8 us (8%)
  other arithmetic  9.28 us (4%)
    ppermute x5, waiting for transfers between devices, passed_along(): lax.ppermute(shard, axis, [(i, (i + by) % peers) for i in range(peers)])  180 us
    ppermute x5, starting transfers between devices, passed_along(): lax.ppermute(shard, axis, [(i, (i + by) % peers) for i in range(peers)])  19.8 us
    dot_general x3, matrix products, score_block(): lax.dot_general(image_block, text_block, (((1,), (1,)), ((), ())), prefer...  8.52 us
    dot_general x3, matrix products, per_device(): lax.dot_general(slopes, image_emb, (((0,), (0,)), ((), ())), preferred_el...  6.58 us
    dot_general x3, matrix products, per_device(): jnp.dot(slopes, current, preferred_element_type=jnp.float32)  6.29 us
    mul x2, other arithmetic, back_norm(): (grad_unit - unit * jnp.sum(unit * grad_unit, axis=1, keepdims=True)) * i...  4.92 us
  transfers between devices with their start and end apart: 5, of which 3 were waited for; matrix products, arithmetic and copies ran while one was open for 7% of the time, Pallas kernels for 0%

commit v1 on v0

v1 whole, which is shorter than its diff:
```python
import jax
import jax.numpy as jnp
from jax import lax
from jax.sharding import PartitionSpec as P

STEPS = 3
EPS = 1e-12


def normalize(raw):
    widened = raw.astype(jnp.float32)
    inverse = lax.rsqrt(jnp.sum(widened * widened, axis=1, keepdims=True) + EPS)
    return (widened * inverse, inverse)


def back_norm(unit, inverse, grad_unit):
    return (grad_unit - unit * jnp.sum(unit * grad_unit, axis=1, keepdims=True)) * inverse


def logits_of(image_emb, text_emb, scale_now, shift_now):
    products = lax.dot_general(
        image_emb, text_emb, (((1,), (1,)), ((), ())), preferred_element_type=jnp.float32
    )
    return scale_now * products + shift_now


def slopes_of(logits, labels, rows):
    return (-labels * jax.nn.sigmoid(-labels * logits) / rows).astype(jnp.bfloat16)


def per_device(images, texts, log_scale, logit_bias):
    count = lax.axis_size("blk")
    odd = lax.axis_index("blk") % 2 == 1
    scale_now = jnp.exp(log_scale[0])
    shift_now = logit_bias[0]
    rows = images.shape[0]

    def send(block, pairs):
        return lax.ppermute(block, "blk", pairs)

    up = [(i, (i + 2) % count) for i in range(count)]
    down = [(i, (i - 2) % count) for i in range(count)]
    across = [(i, i ^ 1) for i in range(count)]
    texts_two = send(texts, up)
    images_two = send(images, down)
    early = send(jnp.where(odd, images, texts), across)
    late = send(jnp.where(odd, texts_two, images_two), across)
    texts_one = jnp.where(odd, early, late)
    images_one = jnp.where(odd, late, early)

    image_unit, image_inverse = normalize(images)
    text_unit, text_inverse = normalize(texts)
    image_emb = image_unit.astype(jnp.bfloat16)
    text_emb = text_unit.astype(jnp.bfloat16)

    logits = logits_of(image_emb, text_emb, scale_now, shift_now)
    labels = jnp.where(jnp.eye(rows, dtype=bool), 1.0, -1.0).astype(jnp.float32)
    loss = jnp.sum(jax.nn.softplus(-labels * logits), axis=1)
    slopes = slopes_of(logits, labels, rows)
    image_acc = scale_now * jnp.dot(slopes, text_emb, preferred_element_type=jnp.float32)
    text_acc = scale_now * lax.dot_general(
        slopes, image_emb, (((0,), (0,)), ((), ())), preferred_element_type=jnp.float32
    )
    for other in (texts_one, texts_two):
        emb = normalize(other)[0].astype(jnp.bfloat16)
        logits = logits_of(image_emb, emb, scale_now, shift_now)
        loss = loss + jnp.sum(jax.nn.softplus(logits), axis=1)
        image_acc = image_acc + scale_now * jnp.dot(
            slopes_of(logits, -1.0, rows), emb, preferred_element_type=jnp.float32
        )
    for other in (images_one, images_two):
        emb = normalize(other)[0].astype(jnp.bfloat16)
        logits = logits_of(text_emb, emb, scale_now, shift_now)
        text_acc = text_acc + scale_now * jnp.dot(
            slopes_of(logits, -1.0, rows), emb, preferred_element_type=jnp.float32
        )
    row_loss = loss / (STEPS * rows)
    return (
        row_loss,
        back_norm(image_unit, image_inverse, image_acc),
        back_norm(text_unit, text_inverse, text_acc),
    )


def solution(mesh):
    placed = (P("blk", None), P("blk", None), P(), P())
    return jax.shard_map(
        per_device,
        mesh=mesh,
        in_specs=placed,
        out_specs=(P("blk"), P("blk", None), P("blk", None)),
        check_vma=False,
    )
```

time: 234 us -> 109 us (0.47)
  waiting for transfers between devices: 180 us -> 26.3 us
  matrix products: 21.4 us -> 47.2 us
  other arithmetic: 9.28 us -> 19.3 us
  starting transfers between devices: 19.8 us -> 13.8 us
    ppermute x5 -> x4, waiting for transfers between devices: 180 us -> 26.3 us  [send(): return lax.ppermute(block, 'blk', pairs)]
    dot_general x6 -> x8, matrix products: 14.8 us -> 43.3 us  [the longest x4 27.2 us: per_device(): jnp.dot(slopes_of(logits, -1.0, rows), emb, preferred_element_type=jnp.fl...]
    ppermute x5 -> x4, starting transfers between devices: 19.8 us -> 13.8 us  [send(): return lax.ppermute(block, 'blk', pairs)]
    reduce_sum x2 -> x5, other arithmetic: 2.43 us -> 6.93 us  [normalize(): inverse = lax.rsqrt(jnp.sum(widened * widened, axis=1, keepdims=True) + EPS)]
    select_n x0 -> x2, other arithmetic: none -> 3.5 us  [the longest x1 1.83 us: per_device(): early = send(jnp.where(odd, images, texts), across)]
    dot_general x3 -> x1, matrix products: 6.58 us -> 3.92 us  [per_device(): lax.dot_general(slopes, image_emb, (((0,), (0,)), ((), ())), preferred_el...]
  transfers between devices with their start and end apart: 5 -> 4, of which waited for: 3 -> 1; matrix products, arithmetic and copies ran while one was open for 7% -> 24% of each run, Pallas kernels for 0% -> 0%
where the time goes in v1:
time: 109 us
  matrix products  47.2 us (43%)
  waiting for transfers between devices  26.3 us (24%)
  other arithmetic  19.3 us (18%)
  starting transfers between devices  13.8 us (13%)
  between operations  2.08 us (2%)
    dot_general x4, matrix products, per_device(): jnp.dot(slopes_of(logits, -1.0, rows), emb, preferred_element_type=jnp.fl...  27.2 us
    ppermute x4, waiting for transfers between devices, send(): return lax.ppermute(block, 'blk', pairs)  26.3 us
    ppermute x4, starting transfers between devices, send(): return lax.ppermute(block, 'blk', pairs)  13.8 us
    dot_general x3, matrix products, logits_of(): lax.dot_general(image_emb, text_emb, (((1,), (1,)), ((), ())), preferred_...  12.4 us
    mul x2, other arithmetic, back_norm(): (grad_unit - unit * jnp.sum(unit * grad_unit, axis=1, keepdims=True)) * i...  7.06 us
    reduce_sum x5, other arithmetic, normalize(): inverse = lax.rsqrt(jnp.sum(widened * widened, axis=1, keepdims=True) + EPS)  6.93 us
    dot_general x1, matrix products, per_device(): lax.dot_general(slopes, image_emb, (((0,), (0,)), ((), ())), preferred_el...  3.92 us
    dot_general x1, matrix products, per_device(): jnp.dot(slopes, text_emb, preferred_element_type=jnp.float32)  3.7 us
  transfers between devices with their start and end apart: 4, of which 1 were waited for; matrix products, arithmetic and copies ran while one was open for 24% of the time, Pallas kernels for 0%

profile of v1, /device:TPU:1, one launch (start us, length us, event | category | flops | bytes accessed | tf_op | source)
XLA Modules:
  0.0 108.7 jit_solution(1521928241733174420)
XLA Ops:
  0.6 2.1 %collective-permute-start.1 = (bf16[768,1152]{1,0:T(8,128)(2,1)}, bf16[768,1152]{1,0:T(8,128)(2,1)}, u32[]{:S(2)}, u32[]{:S(2)}) collective-permute-start(bf16[768,1152]{1,0:T(8,128)(2,1)} %param.5), channel_id=1, source_target_pairs={{0,2},{1,3},{2,4},{3,5},{4,6},{5,7},{6,8},{7,9},{8,10},{9,11},{10,... | collective-permute-start | bytes 5308424 | tf_op jit(solution)/shard_map/ppermute | solution.py:39
  2.7 9.1 %collective-permute-start.2 = (bf16[768,1152]{1,0:T(8,128)(2,1)}, bf16[768,1152]{1,0:T(8,128)(2,1)}, u32[]{:S(2)}, u32[]{:S(2)}) collective-permute-start(bf16[768,1152]{1,0:T(8,128)(2,1)} %param.4), channel_id=1, source_target_pairs={{0,254},{1,255},{2,0},{3,1},{4,2},{5,3},{6,4},{7,5},{8,6},{9,7},{1... | collective-permute-start | bytes 5308424 | tf_op jit(solution)/shard_map/ppermute | solution.py:39
  11.9 1.8 %broadcast_select_fusion.3 = bf16[768,1152]{1,0:T(8,128)(2,1)S(1)} fusion(bf16[768,1152]{1,0:T(8,128)(2,1)} %param.4, bf16[768,1152]{1,0:T(8,128)(2,1)} %param.5, pred[]{:T(512)S(6)} %eq.11), kind=kLoop, calls=%fused_computation.59 | loop fusion | flops 884736 | bytes 5308417 | tf_op jit(solution)/shard_map/jit(_where)/select_n | solution.py:46
  13.7 1.0 collective-permute-start
  16.9 3.5 %fusion.24 = (f32[768]{0:T(1024)}, f32[768,768]{0,1:T(8,128)S(1)}) fusion(f32[]{:T(128)} %bitcast.2, bf16[768,1152]{1,0:T(8,128)(2,1)S(1)} %copy-done, f32[768]{0:T(1024)S(1)} %get-tuple-element.16, bf16[768,1152]{1,0:T(8,128)(2,1)S(1)} %copy-done.1, f32[768]{0:T(1024)S(1)} %get-tuple-element.17, f32[]{:T(128)} %bitcast), kind=kOutput, calls=%fused_computation.43 | convolution fusion | flops 1371929856 | bytes 5907464 | tf_op jit(solution)/shard_map/dot_general | solution.py:21
  20.4 3.7 %fusion.62 = f32[768,1152]{1,0:T(8,128)} fusion(bf16[768,1152]{1,0:T(8,128)(2,1)S(1)} %copy-done, f32[768]{0:T(1024)S(1)} %get-tuple-element.16, f32[768,768]{0,1:T(8,128)S(1)} %get-tuple-element.9), kind=kOutput, calls=%fused_computation.86 | convolution fusion | flops 1366917120 | bytes 7670784 | tf_op jit(solution)/shard_map/dot_general | solution.py:60
  24.1 26.3 %collective-permute-done.1 = bf16[768,1152]{1,0:T(8,128)(2,1)} collective-permute-done((bf16[768,1152]{1,0:T(8,128)(2,1)}, bf16[768,1152]{1,0:T(8,128)(2,1)}, u32[]{:S(2)}, u32[]{:S(2)}) %collective-permute-start.1) | collective-permute-done | bytes 1769504 | tf_op jit(solution)/shard_map/ppermute | solution.py:39
  50.4 1.7 %broadcast_select_fusion.2 = bf16[768,1152]{1,0:T(8,128)(2,1)S(1)} fusion(bf16[768,1152]{1,0:T(8,128)(2,1)} %collective-permute-done.1, bf16[768,1152]{1,0:T(8,128)(2,1)} %collective-permute-done.2, pred[]{:T(512)S(6)} %eq.11), kind=kLoop, calls=%fused_computation.58 | loop fusion | flops 884736 | bytes 5308417 | tf_op jit(solution)/shard_map/jit(_where)/select_n | solution.py:47
  52.1 1.5 %collective-permute-start.3 = (bf16[768,1152]{1,0:T(8,128)(2,1)S(1)}, bf16[768,1152]{1,0:T(8,128)(2,1)S(1)}, u32[]{:S(2)}, u32[]{:S(2)}) collective-permute-start(bf16[768,1152]{1,0:T(8,128)(2,1)S(1)} %broadcast_select_fusion.2), channel_id=1, source_target_pairs={{0,1},{1,0},{2,3},{3,2},{4,5},{5,4},{6,7},{7,6},{8,9},{9,8},{10,11... | collective-permute-start | bytes 5308424 | tf_op jit(solution)/shard_map/ppermute | solution.py:39
  53.6 3.9 %fusion.53 = f32[768,1152]{1,0:T(8,128)} fusion(bf16[768,1152]{1,0:T(8,128)(2,1)S(1)} %copy-done.1, f32[768]{0:T(1024)S(1)} %get-tuple-element.17, f32[768,768]{0,1:T(8,128)S(1)} %get-tuple-element.9), kind=kOutput, calls=%fused_computation.85 | convolution fusion | flops 1366917120 | bytes 7670784 | tf_op jit(solution)/shard_map/dot_general | solution.py:61
  57.5 1.9 %fusion.22 = f32[768]{0:T(1024)S(1)} fusion(bf16[768,1152]{1,0:T(8,128)(2,1)} %collective-permute-done.2), kind=kLoop, calls=%fused_computation.41 | loop fusion | flops 2653440 | bytes 1772544 | tf_op jit(solution)/shard_map/reduce_sum | solution.py:12
  59.4 1.9 %fusion.18 = f32[768]{0:T(1024)S(1)} fusion(bf16[768,1152]{1,0:T(8,128)(2,1)} %collective-permute-done.1), kind=kLoop, calls=%fused_computation.37 | loop fusion | flops 2653440 | bytes 1772544 | tf_op jit(solution)/shard_map/reduce_sum | solution.py:12
  61.3 0.6 add_rsqrt_fusion
  61.9 6.1 %fusion.26 = (f32[768]{0:T(1024)}, f32[768,768]{0,1:T(8,128)}) fusion(f32[]{:T(128)} %bitcast.3, f32[]{:T(128)} %bitcast, bf16[768,1152]{1,0:T(8,128)(2,1)} %collective-permute-done.1, f32[768]{0:T(1024)S(1)} %add_rsqrt_fusion.2, bf16[768,1152]{1,0:T(8,128)(2,1)S(1)} %copy-done.1, f32[768]{0:T(1024)S(1)} %get-tuple-element.17), kind=kOutput, calls=%fused_computation.45 | convolution fusion | flops 1369570560 | bytes 5907464 | tf_op jit(solution)/shard_map/dot_general | solution.py:21
  68.1 2.3 %fusion.16 = (f32[768]{0:T(1024)S(1)}, bf16[768,1152]{1,0:T(8,128)(2,1)}, f32[768]{0:T(1024)S(1)}) fusion(bf16[768,1152]{1,0:T(8,128)(2,1)S(1)} %collective-permute-done, bf16[768,1152]{1,0:T(8,128)(2,1)S(1)} %collective-permute-done.3, pred[]{:T(512)S(6)} %eq.11), kind=kLoop, calls=%fused_computation.35 | loop fusion | flops 7076352 | bytes 5314561 | tf_op jit(solution)/shard_map/reduce_sum | solution.py:12
  70.4 0.6 add_rsqrt_fusion.1
  71.0 10.4 %convolution_add_fusion.1 = f32[768,1152]{1,0:T(8,128)} fusion(f32[768,1152]{1,0:T(8,128)} %fusion.53, f32[]{:T(128)} %bitcast.6, f32[]{:T(128)} %bitcast, f32[768]{0:T(1024)S(1)} %get-tuple-element.18, bf16[768,1152]{1,0:T(8,128)(2,1)} %copy-done.3, bf16[768,1152]{1,0:T(8,128)(2,1)} %copy-done.2, pred[]{:T(512)S(6)} %eq.11, ...), kind=kOutput, calls=%fused_computation.23 | convolution fusion | flops 2732654592 | bytes 12392457 | tf_op jit(solution)/shard_map/dot_general | solution.py:74
  81.4 10.8 %fusion.12 = (f32[768]{0:T(1024)S(1)}, f32[768,1152]{1,0:T(8,128)}) fusion(bf16[768,1152]{1,0:T(8,128)(2,1)S(1)} %copy-done, f32[768]{0:T(1024)S(1)} %get-tuple-element.16, f32[]{:T(128)} %bitcast, f32[768,1152]{1,0:T(8,128)} %convolution_add_fusion.1, bf16[768,1152]{1,0:T(8,128)(2,1)} %collective-permute-done.2, f32[768]{0:T(1024)} %add_rsqrt_fusion, ...), kind=kOutput, calls=%fused_computation.31 | convolution fusion | flops 2735308032 | bytes 10626056 | tf_op jit(solution)/shard_map/dot_general | solution.py:74
  92.2 4.6 %fusion.14 = f32[768,1152]{1,0:T(8,128)} fusion(f32[768,1152]{1,0:T(8,128)} %get-tuple-element.15, bf16[768,1152]{1,0:T(8,128)(2,1)S(1)} %copy-done, f32[768]{0:T(1024)S(1)} %get-tuple-element.14, f32[768]{0:T(1024)S(1)} %get-tuple-element.16), kind=kLoop, calls=%fused_computation.33 | loop fusion | flops 4423680 | bytes 8853504 | tf_op jit(solution)/shard_map/mul | solution.py:17
  96.8 2.8 %fusion.25 = (f32[768]{0:T(1024)S(1)}, f32[768,768]{0,1:T(8,128)S(1)}) fusion(f32[]{:T(128)} %bitcast.4, f32[]{:T(128)} %bitcast, bf16[768,1152]{1,0:T(8,128)(2,1)S(1)} %copy-done.4, f32[768]{0:T(1024)S(1)} %copy-done.7, bf16[768,1152]{1,0:T(8,128)(2,1)S(1)} %copy-done.1, f32[768]{0:T(1024)S(1)} %get-tuple-element.17), kind=kOutput, calls=%fused_computation.44 | convolution fusion | flops 1369570560 | bytes 5907464 | tf_op jit(solution)/shard_map/dot_general | solution.py:21
  99.6 2.0 %convolution_add_fusion.3 = f32[768,1152]{1,0:T(8,128)S(1)} fusion(f32[768,1152]{1,0:T(8,128)S(1)} %copy-done.8, f32[768,768]{0,1:T(8,128)S(1)} %get-tuple-element.11, f32[]{:T(128)} %bitcast.8, f32[]{:T(128)} %bitcast, bf16[768,1152]{1,0:T(8,128)(2,1)S(1)} %copy-done.4, f32[768]{0:T(1024)S(1)} %copy-done.7), kind=kOutput, calls=%fused_computation.26 | convolution fusion | flops 1366622208 | bytes 11209736 | tf_op jit(solution)/shard_map/dot_general | solution.py:68
  101.6 4.0 %fusion.8 = (f32[768]{0:T(1024)S(1)}, f32[768,1152]{1,0:T(8,128)S(1)}) fusion(bf16[768,1152]{1,0:T(8,128)(2,1)S(1)} %copy-done.1, f32[768]{0:T(1024)S(1)} %get-tuple-element.17, f32[]{:T(128)} %bitcast, f32[768,1152]{1,0:T(8,128)S(1)} %convolution_add_fusion.3, bf16[768,1152]{1,0:T(8,128)(2,1)} %collective-permute-done.1, f32[768]{0:T(1024)S(1)} %add_rsqrt_fusion.2, ...), kind=kOutput, calls=%fused_computation.27 | convolution fusion | flops 1371045120 | bytes 12985352 | tf_op jit(solution)/shard_map/dot_general | solution.py:68
  105.7 2.5 %fusion.10 = f32[768,1152]{1,0:T(8,128)} fusion(f32[768,1152]{1,0:T(8,128)S(1)} %get-tuple-element.13, bf16[768,1152]{1,0:T(8,128)(2,1)S(1)} %copy-done.1, f32[768]{0:T(1024)S(1)} %get-tuple-element.12, f32[768]{0:T(1024)S(1)} %get-tuple-element.17), kind=kLoop, calls=%fused_computation.29 | loop fusion | flops 4423680 | bytes 8853504 | tf_op jit(solution)/shard_map/mul | solution.py:17
  108.1 0.6 add_multiply_fusion.1
  (27 shorter events, 0.9 us)
Async XLA Ops:
  0.6 49.8 %collective-permute-start.1 = (bf16[768,1152]{1,0:T(8,128)(2,1)}, bf16[768,1152]{1,0:T(8,128)(2,1)}, u32[]{:S(2)}, u32[]{:S(2)}) collective-permute-start(bf16[768,1152]{1,0:T(8,128)(2,1)} %param.5), channel_id=1, source_target_pairs={{0,2},{1,3},{2,4},{3,5},{4,6},{5,7},{6,8},{7,9},{8,10},{9,11},{10,... | collective-permute-start | bytes 5308424 | tf_op jit(solution)/shard_map/ppermute | solution.py:39
  2.7 47.7 %collective-permute-start.2 = (bf16[768,1152]{1,0:T(8,128)(2,1)}, bf16[768,1152]{1,0:T(8,128)(2,1)}, u32[]{:S(2)}, u32[]{:S(2)}) collective-permute-start(bf16[768,1152]{1,0:T(8,128)(2,1)} %param.4), channel_id=1, source_target_pairs={{0,254},{1,255},{2,0},{3,1},{4,2},{5,3},{6,4},{7,5},{8,6},{9,7},{1... | collective-permute-start | bytes 5308424 | tf_op jit(solution)/shard_map/ppermute | solution.py:39
  11.8 2.9 %copy-start.1 = (bf16[768,1152]{1,0:T(8,128)(2,1)S(1)}, bf16[768,1152]{1,0:T(8,128)(2,1)}, u32[]{:S(2)}) copy-start(bf16[768,1152]{1,0:T(8,128)(2,1)} %param.4) | copy-start | bytes 5308420
  11.8 4.6 %copy-start = (bf16[768,1152]{1,0:T(8,128)(2,1)S(1)}, bf16[768,1152]{1,0:T(8,128)(2,1)}, u32[]{:S(2)}) copy-start(bf16[768,1152]{1,0:T(8,128)(2,1)} %param.5) | copy-start | bytes 5308420
  13.7 54.4 %collective-permute-start = (bf16[768,1152]{1,0:T(8,128)(2,1)S(1)}, bf16[768,1152]{1,0:T(8,128)(2,1)S(1)}, u32[]{:S(2)}, u32[]{:S(2)}) collective-permute-start(bf16[768,1152]{1,0:T(8,128)(2,1)S(1)} %broadcast_select_fusion.3), channel_id=1, source_target_pairs={{0,1},{1,0},{2,3},{3,2},{4,5},{5,4},{6,7},{7,6},{8,9},{9,8},{10,11... | collective-permute-start | bytes 5308424 | tf_op jit(solution)/shard_map/ppermute | solution.py:39
  52.1 16.0 %collective-permute-start.3 = (bf16[768,1152]{1,0:T(8,128)(2,1)S(1)}, bf16[768,1152]{1,0:T(8,128)(2,1)S(1)}, u32[]{:S(2)}, u32[]{:S(2)}) collective-permute-start(bf16[768,1152]{1,0:T(8,128)(2,1)S(1)} %broadcast_select_fusion.2), channel_id=1, source_target_pairs={{0,1},{1,0},{2,3},{3,2},{4,5},{5,4},{6,7},{7,6},{8,9},{9,8},{10,11... | collective-permute-start | bytes 5308424 | tf_op jit(solution)/shard_map/ppermute | solution.py:39
  68.0 2.3 %copy-start.2 = (bf16[768,1152]{1,0:T(8,128)(2,1)}, bf16[768,1152]{1,0:T(8,128)(2,1)S(1)}, u32[]{:S(2)}) copy-start(bf16[768,1152]{1,0:T(8,128)(2,1)S(1)} %collective-permute-done) | copy-start | bytes 5308420
  68.0 2.3 %copy-start.3 = (bf16[768,1152]{1,0:T(8,128)(2,1)}, bf16[768,1152]{1,0:T(8,128)(2,1)S(1)}, u32[]{:S(2)}) copy-start(bf16[768,1152]{1,0:T(8,128)(2,1)S(1)} %collective-permute-done.3) | copy-start | bytes 5308420
  92.2 4.6 %copy-start.4 = (bf16[768,1152]{1,0:T(8,128)(2,1)S(1)}, bf16[768,1152]{1,0:T(8,128)(2,1)}, u32[]{:S(2)}) copy-start(bf16[768,1152]{1,0:T(8,128)(2,1)} %get-tuple-element.4) | copy-start | bytes 5308420
  92.2 4.6 %copy-start.7 = (f32[768]{0:T(1024)S(1)}, f32[768]{0:T(1024)}, u32[]{:S(2)}) copy-start(f32[768]{0:T(1024)} %get-tuple-element.19) | copy-start | bytes 9220
  96.8 2.8 %copy-start.8 = (f32[768,1152]{1,0:T(8,128)S(1)}, f32[768,1152]{1,0:T(8,128)}, u32[]{:S(2)}) copy-start(f32[768,1152]{1,0:T(8,128)} %fusion.62) | copy-start | bytes 10616836
  99.6 2.0 %copy-start.9 = (f32[768,768]{0,1:T(8,128)S(1)}, f32[768,768]{0,1:T(8,128)}, u32[]{:S(2)}) copy-start(f32[768,768]{0,1:T(8,128)} %get-tuple-element.7) | copy-start | bytes 7077892
  105.6 2.5 %copy-start.5 = (f32[768]{0:T(1024)S(1)}, f32[768]{0:T(1024)}, u32[]{:S(2)}) copy-start(f32[768]{0:T(1024)} %get-tuple-element.8) | copy-start | bytes 9220
  105.6 2.5 %copy-start.6 = (f32[768]{0:T(1024)S(1)}, f32[768]{0:T(1024)}, u32[]{:S(2)}) copy-start(f32[768]{0:T(1024)} %get-tuple-element.6) | copy-start | bytes 9220

commit v2 on v1

v2 whole, which is shorter than its diff:
```python
import functools

import jax
import jax.numpy as jnp
from jax import lax
from jax.experimental import pallas as pl
from jax.experimental.pallas import tpu as pltpu
from jax.sharding import PartitionSpec as P

STEPS = 3
EPS = 1e-12
RB = 768
D = 1152
TILE = 256
LANES = 128
PARTS = RB // TILE
VMEM_LIMIT = 12 * 1024 * 1024
CUT = 512
NEAR, FAR = 0, 1

ROWS_BY_COLS = (((1,), (1,)), ((), ()))
TRANSPOSED = (((0,), (0,)), ((), ()))

SCALARS = pl.BlockSpec(memory_space=pltpu.SMEM)
RESIDENT = pl.BlockSpec(memory_space=pltpu.VMEM)
ANYWHERE = pl.BlockSpec(memory_space=pl.ANY)
NO_COST = pl.CostEstimate(flops=1, bytes_accessed=1, transcendentals=0)


def kept(array):
    return pltpu.with_memory_space_constraint(array, pltpu.VMEM)


def tile(part):
    return slice(part * TILE, (part + 1) * TILE)


def normalize(raw):
    widened = raw.astype(jnp.float32)
    inverse = lax.rsqrt(jnp.sum(widened * widened, axis=1, keepdims=True) + EPS)
    return (widened * inverse, inverse)


def matmul(a, b, dims=(((1,), (0,)), ((), ()))):
    return lax.dot_general(a, b, dims, preferred_element_type=jnp.float32)


def scale_row(log_scale, width):
    return jnp.exp(jnp.full((1, width), log_scale[0], jnp.float32))


def lane_sums(values):
    total = values[:, :LANES]
    for start in range(LANES, values.shape[1], LANES):
        total = total + values[:, start : start + LANES]
    return total


def softplus_and_slope(signed):
    raised = jnp.exp(signed)
    slope = raised / ((1.0 + raised) * RB)
    return jnp.log1p(raised), slope


def pick_kernel(odd, images, texts, far, near_head, near_tail, sems):
    def copies(far_block, near_block):
        return [
            pltpu.make_async_copy(far_block, far, sems.at[0]),
            pltpu.make_async_copy(near_block.at[pl.ds(0, CUT)], near_head, sems.at[1]),
            pltpu.make_async_copy(near_block.at[pl.ds(CUT, RB - CUT)], near_tail, sems.at[2]),
        ]

    @pl.when(odd[0] == 1)
    def _():
        for copy in copies(texts, images):
            copy.start()

    @pl.when(odd[0] == 0)
    def _():
        for copy in copies(images, texts):
            copy.start()

    for copy in copies(images, texts):
        copy.wait()


def pick(odd, images, texts):
    return pl.pallas_call(
        pick_kernel,
        in_specs=[SCALARS, ANYWHERE, ANYWHERE],
        out_specs=[RESIDENT] * 3,
        out_shape=[
            pltpu.VMEM((RB, D), jnp.bfloat16),
            pltpu.VMEM((CUT, D), jnp.bfloat16),
            pltpu.VMEM((RB - CUT, D), jnp.bfloat16),
        ],
        scratch_shapes=[pltpu.SemaphoreType.DMA((3,))],
        cost_estimate=NO_COST,
        name="pick",
    )(
        odd,
        pltpu.with_memory_space_constraint(images, pltpu.HBM),
        pltpu.with_memory_space_constraint(texts, pltpu.HBM),
    )


def embed(raw):
    return normalize(raw)[0].astype(jnp.bfloat16)


def prepare_kernel(far, near_head, near_tail, emb):
    for part in range(PARTS):
        emb[FAR, tile(part)] = embed(far[tile(part)])
    for part in range(CUT // TILE):
        emb[NEAR, tile(part)] = embed(near_head[tile(part)])
    emb[NEAR, CUT:] = embed(near_tail[...])


def prepare(far, near_head, near_tail):
    return pl.pallas_call(
        prepare_kernel,
        in_specs=[RESIDENT] * 3,
        out_specs=RESIDENT,
        out_shape=pltpu.VMEM((2, RB, D), jnp.bfloat16),
        compiler_params=pltpu.CompilerParams(vmem_limit_bytes=VMEM_LIMIT),
        cost_estimate=NO_COST,
        name="prepare",
    )(kept(far), kept(near_head), kept(near_tail))


def own_kernel(odd, log_scale, logit_bias, emb, grads, loss, slopes):
    scale_tile, scale_wide = scale_row(log_scale, TILE), scale_row(log_scale, D)
    row_ids = lax.broadcasted_iota(jnp.int32, (TILE, TILE), 0)
    col_ids = lax.broadcasted_iota(jnp.int32, (TILE, TILE), 1)
    images, texts = 1 - odd[0], odd[0]
    for row in range(PARTS):
        losses = jnp.zeros((TILE, LANES), jnp.float32)
        for col in range(PARTS):
            logits = (
                scale_tile * matmul(emb[images, tile(row)], emb[texts, tile(col)], ROWS_BY_COLS)
                + logit_bias[0]
            )
            if row == col:
                same = row_ids == col_ids
                terms, slope = softplus_and_slope(jnp.where(same, -logits, logits))
                slope = jnp.where(same, -slope, slope)
            else:
                terms, slope = softplus_and_slope(logits)
            losses = losses + lane_sums(terms)
            slopes[tile(row), tile(col)] = slope.astype(jnp.bfloat16)
        loss[tile(row)] = losses
        grads[images, tile(row)] = scale_wide * matmul(slopes[tile(row)], emb[texts])
    for col in range(PARTS):
        grads[texts, tile(col)] = scale_wide * matmul(
            slopes[:, tile(col)], emb[images], TRANSPOSED
        )


def own_pairs(odd, log_scale, logit_bias, emb):
    return pl.pallas_call(
        own_kernel,
        in_specs=[SCALARS] * 3 + [RESIDENT],
        out_specs=[RESIDENT] * 2,
        out_shape=[
            pltpu.VMEM((2, RB, D), jnp.float32),
            pltpu.VMEM((RB, LANES), jnp.float32),
        ],
        scratch_shapes=[pltpu.VMEM((RB, RB), jnp.bfloat16)],
        compiler_params=pltpu.CompilerParams(vmem_limit_bytes=VMEM_LIMIT),
        cost_estimate=NO_COST,
        name="own_pairs",
    )(odd, log_scale, logit_bias, kept(emb))


def embed_all(others, other_emb):
    start = 0
    for other in others:
        for part in range(other.shape[0] // TILE):
            other_emb[start : start + TILE] = embed(other[tile(part)])
            start += TILE


def score(row, side, has_loss, log_scale, logit_bias, emb, loss_in, loss, other_emb, slopes):
    scale_tile = scale_row(log_scale, TILE)
    losses = jnp.zeros((TILE, LANES), jnp.float32)
    for col in range(other_emb.shape[0] // TILE):
        logits = (
            scale_tile * matmul(emb[side, tile(row)], other_emb[tile(col)], ROWS_BY_COLS)
            + logit_bias[0]
        )
        terms, slope = softplus_and_slope(logits)
        losses = losses + lane_sums(terms)
        slopes[tile(row), tile(col)] = slope.astype(jnp.bfloat16)
    loss[tile(row)] = loss_in[tile(row)] + jnp.where(has_loss, losses, 0.0)
    return scale_row(log_scale, D) * matmul(slopes[tile(row)], other_emb[...])


def add_kernel(*refs, side, pieces):
    odd, log_scale, logit_bias, *others = refs[: 3 + pieces]
    emb, grads_in, loss_in, grads, loss, other_emb, slopes = refs[3 + pieces :]
    embed_all(others, other_emb)
    has_loss = odd[0] == (1 if side == NEAR else 0)
    for row in range(PARTS):
        addend = score(
            row, side, has_loss, log_scale, logit_bias, emb, loss_in, loss, other_emb, slopes
        )
        grads[side, tile(row)] = grads_in[side, tile(row)] + addend


def finish_kernel(*refs, side, raws):
    odd, log_scale, logit_bias, other, emb, grads, loss_in = refs[:7]
    raw = refs[7 : 7 + raws]
    tail = refs[7 + raws + (2 if side == FAR else 0) :]
    result, image_grad, text_grad, other_emb, slopes, finished, sems = tail
    embed_all([other], other_emb)
    has_loss = odd[0] == (1 if side == NEAR else 0)
    loss = result
    for row in range(PARTS):
        here = tile(row)
        addend = score(
            row, side, has_loss, log_scale, logit_bias, emb, loss_in, loss, other_emb, slopes
        )
        total = grads[side, here] + addend
        if raws == 1:
            mine = raw[0][here]
        else:
            mine = raw[0][here] if row * TILE < CUT else raw[1][tile(row - CUT // TILE)]
        unit, inverse = normalize(mine)
        finished[here] = (total - unit * jnp.sum(unit * total, axis=1, keepdims=True)) * inverse

        @pl.when(odd[0] == (1 if side == NEAR else 0))
        def _(here=here, row=row):
            pltpu.make_async_copy(finished.at[here], image_grad.at[here], sems.at[row]).start()

        @pl.when(odd[0] == (0 if side == NEAR else 1))
        def _(here=here, row=row):
            pltpu.make_async_copy(finished.at[here], text_grad.at[here], sems.at[row]).start()

    for row in range(PARTS):
        here = tile(row)
        pltpu.make_async_copy(finished.at[here], image_grad.at[here], sems.at[row]).wait()


def score_scratch(count):
    return [pltpu.VMEM((count, D), jnp.bfloat16), pltpu.VMEM((RB, count), jnp.bfloat16)]


def add_pairs(side, scalars, others, emb, grads, loss):
    count = sum(other.shape[0] for other in others)
    at = 4 + len(others)
    return pl.pallas_call(
        functools.partial(add_kernel, side=side, pieces=len(others)),
        in_specs=[SCALARS] * 3 + [RESIDENT] * (3 + len(others)),
        out_specs=[RESIDENT] * 2,
        out_shape=[
            pltpu.VMEM(grads.shape, jnp.float32),
            pltpu.VMEM(loss.shape, jnp.float32),
        ],
        scratch_shapes=score_scratch(count),
        input_output_aliases={at: 0, at + 1: 1},
        compiler_params=pltpu.CompilerParams(vmem_limit_bytes=VMEM_LIMIT),
        cost_estimate=NO_COST,
        name="add_pairs",
    )(*scalars, *map(kept, others), kept(emb), kept(grads), kept(loss))


def finish_pairs(side, scalars, other, emb, grads, loss, raws, outs=()):
    count = other.shape[0]
    aliases = {6: 0}
    if outs:
        aliases |= {7 + len(raws): 1, 8 + len(raws): 2}
    return pl.pallas_call(
        functools.partial(finish_kernel, side=side, raws=len(raws)),
        in_specs=[SCALARS] * 3 + [RESIDENT] * (4 + len(raws)) + [ANYWHERE] * len(outs),
        out_specs=[RESIDENT, ANYWHERE, ANYWHERE],
        out_shape=[
            pltpu.VMEM(loss.shape, jnp.float32),
            jax.ShapeDtypeStruct((RB, D), jnp.float32),
            jax.ShapeDtypeStruct((RB, D), jnp.float32),
        ],
        scratch_shapes=score_scratch(count)
        + [
            pltpu.VMEM((RB, D), jnp.float32),
            pltpu.SemaphoreType.DMA((PARTS,)),
        ],
        input_output_aliases=aliases,
        compiler_params=pltpu.CompilerParams(vmem_limit_bytes=VMEM_LIMIT),
        cost_estimate=NO_COST,
        name="finish_pairs",
    )(*scalars, kept(other), kept(emb), kept(grads), kept(loss), *map(kept, raws), *outs)


def per_device(images, texts, log_scale, logit_bias):
    count = lax.axis_size("blk")
    odd = (lax.axis_index("blk") % 2).astype(jnp.int32)[None]
    scalars = (odd, log_scale, logit_bias)

    first = [(i, (i + 2) % count if i % 2 else (i - 2) % count) for i in range(count)]
    second = [(i, (i + 1) % count if i % 2 else (i - 1) % count) for i in range(count)]
    across = [(i, i ^ 1) for i in range(count)]

    def send(block, pairs):
        return lax.ppermute(block, "blk", pairs)

    far, near_head, near_tail = pick(odd, images, texts)
    far_other = send(far, first)
    beside_head = send(near_head, across)
    beside_tail = send(near_tail, across)
    emb = prepare(far, near_head, near_tail)
    beside_head, beside_tail, emb = lax.optimization_barrier((beside_head, beside_tail, emb))
    near_head_other = send(beside_head, second)
    near_tail_other = send(beside_tail, second)
    grads, loss = own_pairs(*scalars, emb)
    grads, loss = add_pairs(NEAR, scalars, [beside_head, beside_tail], emb, grads, loss)
    far_other, grads = lax.optimization_barrier((far_other, grads))
    far_beside = [send(far_other[start : start + TILE], across) for start in range(0, RB, TILE)]
    loss, *outs = finish_pairs(
        NEAR, scalars, far_other, emb, grads, loss, [near_head, near_tail]
    )
    grads, loss = add_pairs(FAR, scalars, far_beside, emb, grads, loss)
    grads, loss = add_pairs(FAR, scalars, [near_head_other], emb, grads, loss)
    loss, image_grad, text_grad = finish_pairs(
        FAR, scalars, near_tail_other, emb, grads, loss, [far], outs
    )
    row_loss = jnp.sum(loss, axis=1) / (STEPS * RB)
    return (row_loss, image_grad, text_grad)


def solution(mesh):
    placed = (P("blk", None), P("blk", None), P(), P())
    return jax.shard_map(
        per_device,
        mesh=mesh,
        in_specs=placed,
        out_specs=(P("blk"), P("blk", None), P("blk", None)),
        check_vma=False,
    )
```

time: 109 us -> 63.5 us (0.58)
  the two profiles are of different devices: /device:TPU:1 before, /device:TPU:0 now
where the time goes in v2:
time: 63.5 us; the launch traced here: 63.3 us
  Pallas kernels  36.9 us (58%)
  starting transfers between devices  18.4 us (29%)
  waiting for transfers between devices  5.04 us (8%)
  between operations  2.05 us (3%)
  other arithmetic  0.77 us (1%)
    ppermute x8, starting transfers between devices, send(): return lax.ppermute(block, 'blk', pairs)  18.4 us
    pallas_call x3, Pallas kernels, add_pairs(): pl.pallas_call(functools.partial(add_kernel, side=side, pieces=len(others...  13.2 us
    pallas_call x2, Pallas kernels, finish_pairs(): pl.pallas_call(functools.partial(finish_kernel, side=side, raws=len(raws)...  12.3 us
    pallas_call x1, Pallas kernels, own_pairs(): pl.pallas_call(own_kernel, in_specs=[SCALARS] * 3 + [RESIDENT], out_specs...  5.59 us
    ppermute x8, waiting for transfers between devices, send(): return lax.ppermute(block, 'blk', pairs)  5.04 us
    pallas_call x1, Pallas kernels, pick(): pl.pallas_call(pick_kernel, in_specs=[SCALARS, ANYWHERE, ANYWHERE], out_s...  3.21 us
    pallas_call x1, Pallas kernels, prepare(): pl.pallas_call(prepare_kernel, in_specs=[RESIDENT] * 3, out_specs=RESIDEN...  2.58 us
  transfers between devices with their start and end apart: 8, of which 2 were waited for; matrix products, arithmetic and copies ran while one was open for 0% of the time, Pallas kernels for 44%

profile of v2, /device:TPU:0, one launch (start us, length us, event | category | flops | bytes accessed | tf_op | source)
XLA Modules:
  0.0 63.3 jit_solution(4165981413636552480)
XLA Ops:
  0.6 3.2 %pick.1 = (bf16[768,1152]{1,0:T(8,128)(2,1)}, bf16[512,1152]{1,0:T(8,128)(2,1)S(1)}, bf16[256,1152]{1,0:T(8,128)(2,1)S(1)}) custom-call(s32[1]{0:T(128)} %bitcast.odd.refs_0_, bf16[768,1152]{1,0:T(8,128)(2,1)} %images.1, bf16[768,1152]{1,0:T(8,128)(2,1)} %texts.1), custom_call_target="tpu_custom_call" | custom-call | flops 1 | bytes 1 | tf_op jit(solution)/shard_map/pick/pallas_call | solution.py:88
  3.9 8.8 %collective-permute-start.4 = (bf16[768,1152]{1,0:T(8,128)(2,1)}, bf16[768,1152]{1,0:T(8,128)(2,1)S(1)}, u32[]{:S(2)}, u32[]{:S(2)}) collective-permute-start(bf16[768,1152]{1,0:T(8,128)(2,1)} %get-tuple-element.27.far.refs_7_), channel_id=1, source_target_pairs={{0,254},{1,3},{2,0},{3,5},{4,2},{5,7},{6,4},{7,9},{8,6},{9,11},{10... | collective-permute-start | bytes 5308424 | tf_op jit(solution)/shard_map/ppermute | solution.py:303
  12.7 0.0 collective-permute-start
  12.7 0.5 collective-permute-start.1
  13.2 2.6 %prepare.1.emb.refs_5_.refs_4_.refs_6_ = bf16[2,768,1152]{2,1,0:T(8,128)(2,1)S(1)} custom-call(bf16[768,1152]{1,0:T(8,128)(2,1)} %get-tuple-element.27.far.refs_7_, bf16[512,1152]{1,0:T(8,128)(2,1)S(1)} %get-tuple-element.25.near_head.refs_7_, bf16[256,1152]{1,0:T(8,128)(2,1)S(1)} %get-tuple-element.26.near_tail.refs_8_), custom_call_target="tpu_custom_call" | custom-call | flops 1 | bytes 1 | tf_op jit(solution)/shard_map/prepare/pallas_call | solution.py:120
  15.8 0.6 collective-permute-done.1.refs_4_
  16.4 0.6 collective-permute-start.3
  18.3 5.6 %own_pairs.1 = (f32[2,768,1152]{2,1,0:T(8,128)S(1)}, f32[768,128]{1,0:T(8,128)S(1)}) custom-call(s32[1]{0:T(128)} %bitcast.odd.refs_0_, f32[1]{0:T(128)S(6)} %copy.27.log_scale.refs_1_, f32[1]{0:T(128)S(6)} %copy.28.logit_bias.refs_2_, bf16[2,768,1152]{2,1,0:T(8,128)(2,1)S(1)} %prepare.1.emb.refs_5_.refs_4_.refs_6_), custom_call_target="tpu_custom_call" | custom-call | flops 1 | bytes 1 | tf_op jit(solution)/shard_map/own_pairs/pallas_call | solution.py:160
  23.9 4.8 %add_pairs.3 = (f32[2,768,1152]{2,1,0:T(8,128)S(1)}, f32[768,128]{1,0:T(8,128)S(1)}) custom-call(s32[1]{0:T(128)} %bitcast.odd.refs_0_, f32[1]{0:T(128)S(6)} %copy.27.log_scale.refs_1_, f32[1]{0:T(128)S(6)} %copy.28.logit_bias.refs_2_, bf16[512,1152]{1,0:T(8,128)(2,1)S(1)} %collective-permute-done.refs_3_, ...), custom_call_target="tpu_custom_call", output_to_operand_aliasing={{0}: (6, {}), {1}: (7, {})} | custom-call | flops 1 | bytes 1 | tf_op jit(solution)/shard_map/add_pairs/pallas_call | solution.py:251
  28.6 4.4 %collective-permute-done.4.refs_3_ = bf16[768,1152]{1,0:T(8,128)(2,1)S(1)} collective-permute-done((bf16[768,1152]{1,0:T(8,128)(2,1)}, bf16[768,1152]{1,0:T(8,128)(2,1)S(1)}, u32[]{:S(2)}, u32[]{:S(2)}) %collective-permute-start.4) | collective-permute-done | bytes 1769504 | tf_op jit(solution)/shard_map/ppermute | solution.py:303
  33.1 0.1 fusion
  33.2 0.1 collective-permute-start.7
  33.3 0.5 collective-permute-start.6
  33.8 0.1 collective-permute-start.5
  33.9 7.8 %collective-permute-start.2 = (bf16[256,1152]{1,0:T(8,128)(2,1)S(1)}, bf16[256,1152]{1,0:T(8,128)(2,1)S(1)}, u32[]{:S(2)}, u32[]{:S(2)}) collective-permute-start(bf16[256,1152]{1,0:T(8,128)(2,1)S(1)} %collective-permute-done.1.refs_4_), channel_id=1, source_target_pairs={{0,255},{1,2},{2,1},{3,4},{4,3},{5,6},{6,5},{7,8},{8,7},{9,10},{10... | collective-permute-start | bytes 1769480 | tf_op jit(solution)/shard_map/ppermute | solution.py:303
  41.7 6.6 %finish_pairs.2 = (f32[768,128]{1,0:T(8,128)S(1)}, f32[768,1152]{1,0:T(8,128)}, f32[768,1152]{1,0:T(8,128)}) custom-call(s32[1]{0:T(128)} %bitcast.odd.refs_0_, f32[1]{0:T(128)S(6)} %copy.27.log_scale.refs_1_, f32[1]{0:T(128)S(6)} %copy.28.logit_bias.refs_2_, bf16[768,1152]{1,0:T(8,128)(2,1)S(1)} %collective-permute-done.4.refs_3_, ...), custom_call_target="tpu_custom_call", output_to_operand_aliasing={{0}: (6, {})} | custom-call | flops 1 | bytes 1 | tf_op jit(solution)/shard_map/finish_pairs/pallas_call | solution.py:272
  48.3 0.0 collective-permute-done.7.refs_5_
  48.3 0.0 collective-permute-done.6.refs_4_
  48.4 4.8 %add_pairs.4 = (f32[2,768,1152]{2,1,0:T(8,128)S(1)}, f32[768,128]{1,0:T(8,128)S(1)}) custom-call(s32[1]{0:T(128)} %bitcast.odd.refs_0_, f32[1]{0:T(128)S(6)} %copy.27.log_scale.refs_1_, f32[1]{0:T(128)S(6)} %copy.28.logit_bias.refs_2_, bf16[256,1152]{1,0:T(8,128)(2,1)S(1)} %collective-permute-done.5.refs_3_, ...), custom_call_target="tpu_custom_call", output_to_operand_aliasing={{0}: (7, {}), {1}: (8, {})} | custom-call | flops 1 | bytes 1 | tf_op jit(solution)/shard_map/add_pairs/pallas_call | solution.py:251
  53.1 0.0 collective-permute-done.3.refs_3_
  53.2 3.6 %add_pairs.5 = (f32[2,768,1152]{2,1,0:T(8,128)S(1)}, f32[768,128]{1,0:T(8,128)S(1)}) custom-call(s32[1]{0:T(128)} %bitcast.odd.refs_0_, f32[1]{0:T(128)S(6)} %copy.27.log_scale.refs_1_, f32[1]{0:T(128)S(6)} %copy.28.logit_bias.refs_2_, bf16[512,1152]{1,0:T(8,128)(2,1)S(1)} %collective-permute-done.3.refs_3_, ...), custom_call_target="tpu_custom_call", output_to_operand_aliasing={{0}: (5, {}), {1}: (6, {})} | custom-call | flops 1 | bytes 1 | tf_op jit(solution)/shard_map/add_pairs/pallas_call | solution.py:251
  56.8 5.7 %finish_pairs.3 = (f32[768,128]{1,0:T(8,128)S(1)}, f32[768,1152]{1,0:T(8,128)}, f32[768,1152]{1,0:T(8,128)}) custom-call(s32[1]{0:T(128)} %bitcast.odd.refs_0_, f32[1]{0:T(128)S(6)} %copy.27.log_scale.refs_1_, f32[1]{0:T(128)S(6)} %copy.28.logit_bias.refs_2_, ...), custom_call_target="tpu_custom_call", output_to_operand_aliasing={{0}: (6, {}), {1}: (8, {}), {2}: (9, {})} | custom-call | flops 1 | bytes 1 | tf_op jit(solution)/shard_map/finish_pairs/pallas_call | solution.py:272
  62.5 0.2 reduce_sum.9
  62.7 0.6 broadcast_multiply_fusion
  (3 shorter events, 0.0 us)
Async XLA Ops:
  3.9 29.2 %collective-permute-start.4 = (bf16[768,1152]{1,0:T(8,128)(2,1)}, bf16[768,1152]{1,0:T(8,128)(2,1)S(1)}, u32[]{:S(2)}, u32[]{:S(2)}) collective-permute-start(bf16[768,1152]{1,0:T(8,128)(2,1)} %get-tuple-element.27.far.refs_7_), channel_id=1, source_target_pairs={{0,254},{1,3},{2,0},{3,5},{4,2},{5,7},{6,4},{7,9},{8,6},{9,11},{10... | collective-permute-start | bytes 5308424 | tf_op jit(solution)/shard_map/ppermute | solution.py:303
  12.7 3.7 %collective-permute-start = (bf16[512,1152]{1,0:T(8,128)(2,1)S(1)}, bf16[512,1152]{1,0:T(8,128)(2,1)S(1)}, u32[]{:S(2)}, u32[]{:S(2)}) collective-permute-start(bf16[512,1152]{1,0:T(8,128)(2,1)S(1)} %get-tuple-element.25.near_head.refs_7_), channel_id=1, source_target_pairs={{0,1},{1,0},{2,3},{3,2},{4,5},{5,4},{6,7},{7,6},{8,9},{9,8},{10,11... | collective-permute-start | bytes 3538952 | tf_op jit(solution)/shard_map/ppermute | solution.py:303
  12.7 3.7 %collective-permute-start.1 = (bf16[256,1152]{1,0:T(8,128)(2,1)S(1)}, bf16[256,1152]{1,0:T(8,128)(2,1)S(1)}, u32[]{:S(2)}, u32[]{:S(2)}) collective-permute-start(bf16[256,1152]{1,0:T(8,128)(2,1)S(1)} %get-tuple-element.26.near_tail.refs_8_), channel_id=1, source_target_pairs={{0,1},{1,0},{2,3},{3,2},{4,5},{5,4},{6,7},{7,6},{8,9},{9,8},{10,11... | collective-permute-start | bytes 1769480 | tf_op jit(solution)/shard_map/ppermute | solution.py:303
  16.4 36.7 %collective-permute-start.3 = (bf16[512,1152]{1,0:T(8,128)(2,1)S(1)}, bf16[512,1152]{1,0:T(8,128)(2,1)S(1)}, u32[]{:S(2)}, u32[]{:S(2)}) collective-permute-start(bf16[512,1152]{1,0:T(8,128)(2,1)S(1)} %collective-permute-done.refs_3_), channel_id=1, source_target_pairs={{0,255},{1,2},{2,1},{3,4},{4,3},{5,6},{6,5},{7,8},{8,7},{9,10},{10... | collective-permute-start | bytes 3538952 | tf_op jit(solution)/shard_map/ppermute | solution.py:303
  33.2 15.1 %collective-permute-start.7 = (bf16[256,1152]{1,0:T(8,128)(2,1)S(1)}, bf16[256,1152]{1,0:T(8,128)(2,1)S(1)}, u32[]{:S(2)}, u32[]{:S(2)}) collective-permute-start(bf16[256,1152]{1,0:T(8,128)(2,1)S(1)} %get-tuple-element.47), channel_id=1, source_target_pairs={{0,1},{1,0},{2,3},{3,2},{4,5},{5,4},{6,7},{7,6},{8,9},{9,8},{10,11... | collective-permute-start | bytes 1769480 | tf_op jit(solution)/shard_map/ppermute | solution.py:303
  33.3 15.0 %collective-permute-start.6 = (bf16[256,1152]{1,0:T(8,128)(2,1)S(1)}, bf16[256,1152]{1,0:T(8,128)(2,1)S(1)}, u32[]{:S(2)}, u32[]{:S(2)}) collective-permute-start(bf16[256,1152]{1,0:T(8,128)(2,1)S(1)} %get-tuple-element.48), channel_id=1, source_target_pairs={{0,1},{1,0},{2,3},{3,2},{4,5},{5,4},{6,7},{7,6},{8,9},{9,8},{10,11... | collective-permute-start | bytes 1769480 | tf_op jit(solution)/shard_map/ppermute | solution.py:303
  33.8 14.6 %collective-permute-start.5 = (bf16[256,1152]{1,0:T(8,128)(2,1)S(1)}, bf16[256,1152]{1,0:T(8,128)(2,1)S(1)}, u32[]{:S(2)}, u32[]{:S(2)}) collective-permute-start(bf16[256,1152]{1,0:T(8,128)(2,1)S(1)} %get-tuple-element.49), channel_id=1, source_target_pairs={{0,1},{1,0},{2,3},{3,2},{4,5},{5,4},{6,7},{7,6},{8,9},{9,8},{10,11... | collective-permute-start | bytes 1769480 | tf_op jit(solution)/shard_map/ppermute | solution.py:303
  33.9 22.9 %collective-permute-start.2 = (bf16[256,1152]{1,0:T(8,128)(2,1)S(1)}, bf16[256,1152]{1,0:T(8,128)(2,1)S(1)}, u32[]{:S(2)}, u32[]{:S(2)}) collective-permute-start(bf16[256,1152]{1,0:T(8,128)(2,1)S(1)} %collective-permute-done.1.refs_4_), channel_id=1, source_target_pairs={{0,255},{1,2},{2,1},{3,4},{4,3},{5,6},{6,5},{7,8},{8,7},{9,10},{10... | collective-permute-start | bytes 1769480 | tf_op jit(solution)/shard_map/ppermute | solution.py:303

commit v3 on v2

v3 whole, which is shorter than its diff:
```python
import functools

import jax
import jax.numpy as jnp
from jax import lax
from jax.experimental import pallas as pl
from jax.experimental.pallas import tpu as pltpu
from jax.sharding import PartitionSpec as P

STEPS = 3
EPS = 1e-12
RB = 768
D = 1152
TILE = 256
LANES = 128
PARTS = RB // TILE
VMEM_LIMIT = 12 * 1024 * 1024
CUT = 400
PIECE = 256
NEAR, FAR = 0, 1

ROWS_BY_COLS = (((1,), (1,)), ((), ()))
TRANSPOSED = (((0,), (0,)), ((), ()))

SCALARS = pl.BlockSpec(memory_space=pltpu.SMEM)
RESIDENT = pl.BlockSpec(memory_space=pltpu.VMEM)
ANYWHERE = pl.BlockSpec(memory_space=pl.ANY)
NO_COST = pl.CostEstimate(flops=1, bytes_accessed=1, transcendentals=0)


def kept(array):
    return pltpu.with_memory_space_constraint(array, pltpu.VMEM)


def in_hbm(array):
    return pltpu.with_memory_space_constraint(array, pltpu.HBM)


def tile(part):
    return slice(part * TILE, (part + 1) * TILE)


def normalize(raw):
    widened = raw.astype(jnp.float32)
    inverse = lax.rsqrt(jnp.sum(widened * widened, axis=1, keepdims=True) + EPS)
    return (widened * inverse, inverse)


def matmul(a, b, dims=(((1,), (0,)), ((), ()))):
    return lax.dot_general(a, b, dims, preferred_element_type=jnp.float32)


def scale_row(log_scale, width):
    return jnp.exp(jnp.full((1, width), log_scale[0], jnp.float32))


def lane_sums(values):
    total = values[:, :LANES]
    for start in range(LANES, values.shape[1], LANES):
        total = total + values[:, start : start + LANES]
    return total


def softplus_and_slope(signed):
    raised = jnp.exp(signed)
    slope = raised / ((1.0 + raised) * RB)
    return jnp.log1p(raised), slope


def copy_if(condition, source, target, sem):
    @pl.when(condition)
    def _():
        pltpu.make_async_copy(source, target, sem).start()


def pick_kernel(odd, images, texts, far, sem):
    copy_if(odd[0] == 1, texts, far, sem)
    copy_if(odd[0] == 0, images, far, sem)
    pltpu.make_async_copy(images, far, sem).wait()


def pick(odd, images, texts):
    return pl.pallas_call(
        pick_kernel,
        in_specs=[SCALARS, ANYWHERE, ANYWHERE],
        out_specs=RESIDENT,
        out_shape=pltpu.VMEM((RB, D), jnp.bfloat16),
        scratch_shapes=[pltpu.SemaphoreType.DMA],
        cost_estimate=NO_COST,
        name="pick",
    )(odd, in_hbm(images), in_hbm(texts))


def embed(raw):
    return normalize(raw)[0].astype(jnp.bfloat16)


def prepare_kernel(odd, images, texts, far, emb, near_head, near_tail, sems):
    head, tail = pl.ds(0, CUT), pl.ds(CUT, RB - CUT)
    copy_if(odd[0] == 1, images.at[head], near_head, sems.at[0])
    copy_if(odd[0] == 0, texts.at[head], near_head, sems.at[0])
    copy_if(odd[0] == 1, images.at[tail], near_tail, sems.at[1])
    copy_if(odd[0] == 0, texts.at[tail], near_tail, sems.at[1])
    for part in range(PARTS):
        emb[FAR, tile(part)] = embed(far[tile(part)])
    pltpu.make_async_copy(images.at[head], near_head, sems.at[0]).wait()
    pltpu.make_async_copy(images.at[tail], near_tail, sems.at[1]).wait()
    emb[NEAR, :CUT] = embed(near_head[...])
    emb[NEAR, CUT:] = embed(near_tail[...])


def prepare(odd, images, texts, far):
    return pl.pallas_call(
        prepare_kernel,
        in_specs=[SCALARS, ANYWHERE, ANYWHERE, RESIDENT],
        out_specs=[RESIDENT] * 3,
        out_shape=[
            pltpu.VMEM((2, RB, D), jnp.bfloat16),
            pltpu.VMEM((CUT, D), jnp.bfloat16),
            pltpu.VMEM((RB - CUT, D), jnp.bfloat16),
        ],
        scratch_shapes=[pltpu.SemaphoreType.DMA((2,))],
        compiler_params=pltpu.CompilerParams(vmem_limit_bytes=VMEM_LIMIT),
        cost_estimate=NO_COST,
        name="prepare",
    )(odd, in_hbm(images), in_hbm(texts), kept(far))


def own_kernel(odd, log_scale, logit_bias, emb, grads, loss, slopes):
    scale_tile, scale_wide = scale_row(log_scale, TILE), scale_row(log_scale, D)
    row_ids = lax.broadcasted_iota(jnp.int32, (TILE, TILE), 0)
    col_ids = lax.broadcasted_iota(jnp.int32, (TILE, TILE), 1)
    images, texts = 1 - odd[0], odd[0]
    for row in range(PARTS):
        losses = jnp.zeros((TILE, LANES), jnp.float32)
        for col in range(PARTS):
            logits = (
                scale_tile * matmul(emb[images, tile(row)], emb[texts, tile(col)], ROWS_BY_COLS)
                + logit_bias[0]
            )
            if row == col:
                same = row_ids == col_ids
                terms, slope = softplus_and_slope(jnp.where(same, -logits, logits))
                slope = jnp.where(same, -slope, slope)
            else:
                terms, slope = softplus_and_slope(logits)
            losses = losses + lane_sums(terms)
            slopes[tile(row), tile(col)] = slope.astype(jnp.bfloat16)
        loss[tile(row)] = losses
        grads[images, tile(row)] = scale_wide * matmul(slopes[tile(row)], emb[texts])
    for col in range(PARTS):
        grads[texts, tile(col)] = scale_wide * matmul(
            slopes[:, tile(col)], emb[images], TRANSPOSED
        )


def own_pairs(odd, log_scale, logit_bias, emb):
    return pl.pallas_call(
        own_kernel,
        in_specs=[SCALARS] * 3 + [RESIDENT],
        out_specs=[RESIDENT] * 2,
        out_shape=[
            pltpu.VMEM((2, RB, D), jnp.float32),
            pltpu.VMEM((RB, LANES), jnp.float32),
        ],
        scratch_shapes=[pltpu.VMEM((RB, RB), jnp.bfloat16)],
        compiler_params=pltpu.CompilerParams(vmem_limit_bytes=VMEM_LIMIT),
        cost_estimate=NO_COST,
        name="own_pairs",
    )(odd, log_scale, logit_bias, kept(emb))


def padded(count):
    return -(-count // LANES) * LANES


def embed_all(others, other_emb):
    start = 0
    for other in others:
        count = other.shape[0]
        for at in range(0, count, LANES):
            step = min(LANES, count - at)
            other_emb[start : start + step] = embed(other[at : at + step])
            start += step
    if start < other_emb.shape[0]:
        other_emb[start:] = jnp.zeros((other_emb.shape[0] - start, D), jnp.bfloat16)
    return start


def score(side, has_loss, log_scale, logit_bias, emb, loss_in, loss, other_emb, slopes, valid):
    count = other_emb.shape[0]
    step = RB if count == RB else TILE
    for row in range(0, RB, step):
        rows = slice(row, row + step)
        losses = jnp.zeros((step, LANES), jnp.float32)
        for start in range(0, count, TILE):
            cols = slice(start, min(start + TILE, count))
            width = cols.stop - start
            logits = (
                scale_row(log_scale, width)
                * matmul(emb[side, rows], other_emb[cols], ROWS_BY_COLS)
                + logit_bias[0]
            )
            terms, slope = softplus_and_slope(logits)
            if cols.stop > valid:
                ids = lax.broadcasted_iota(jnp.int32, (step, width), 1)
                terms = jnp.where(ids < valid - start, terms, 0.0)
            losses = losses + lane_sums(terms)
            slopes[rows, cols] = slope.astype(jnp.bfloat16)
        loss[rows] = loss_in[rows] + jnp.where(has_loss, losses, 0.0)


def add_kernel(*refs, side, pieces):
    odd, log_scale, logit_bias, *others = refs[: 3 + pieces]
    emb, grads_in, loss_in, grads, loss, other_emb, slopes = refs[3 + pieces :]
    valid = embed_all(others, other_emb)
    has_loss = odd[0] == (1 if side == NEAR else 0)
    score(side, has_loss, log_scale, logit_bias, emb, loss_in, loss, other_emb, slopes, valid)
    scale_wide = scale_row(log_scale, D)
    step = RB if other_emb.shape[0] == RB else TILE
    for row in range(0, RB, step):
        rows = slice(row, row + step)
        grads[side, rows] = grads_in[side, rows] + scale_wide * matmul(
            slopes[rows], other_emb[...]
        )


def finish_kernel(*refs, side):
    odd, log_scale, logit_bias, other, emb, grads, loss_in, images, texts = refs[:9]
    if side == FAR:
        refs = refs[2:]
    loss, image_grad, text_grad, *scratch = refs[9:]
    other_emb, slopes, raw, finished, raw_sem, out_sems = scratch[:6]
    of_images = odd[0] == (1 if side == NEAR else 0)
    copy_if(of_images, images, raw, raw_sem)
    copy_if(jnp.logical_not(of_images), texts, raw, raw_sem)
    valid = embed_all([other], other_emb)
    sums = loss if side == NEAR else scratch[6]
    score(side, of_images, log_scale, logit_bias, emb, loss_in, sums, other_emb, slopes, valid)
    scale_wide = scale_row(log_scale, D)

    def accumulate(rows):
        finished[rows] = grads[side, rows] + scale_wide * matmul(slopes[rows], other_emb[...])

    def finish(here):
        total = finished[here]
        unit, inverse = normalize(raw[here])
        finished[here] = (total - unit * jnp.sum(unit * total, axis=1, keepdims=True)) * inverse

    if side == NEAR:
        accumulate(slice(0, RB))
    pltpu.make_async_copy(images, raw, raw_sem).wait()
    for row in range(PARTS):
        here = tile(row)
        if side == FAR:
            accumulate(here)
        finish(here)
        copy_if(of_images, finished.at[here], image_grad.at[here], out_sems.at[row])
        copy_if(
            jnp.logical_not(of_images), finished.at[here], text_grad.at[here], out_sems.at[row]
        )
    if side == FAR:
        for row in range(PARTS):
            loss[tile(row)] = jnp.sum(sums[tile(row)].T, axis=0) * (1.0 / (STEPS * RB))
    for row in range(PARTS):
        here = tile(row)
        pltpu.make_async_copy(finished.at[here], image_grad.at[here], out_sems.at[row]).wait()


def score_scratch(count):
    return [
        pltpu.VMEM((padded(count), D), jnp.bfloat16),
        pltpu.VMEM((RB, padded(count)), jnp.bfloat16),
    ]


def add_pairs(side, scalars, others, emb, grads, loss):
    count = sum(other.shape[0] for other in others)
    at = 4 + len(others)
    return pl.pallas_call(
        functools.partial(add_kernel, side=side, pieces=len(others)),
        in_specs=[SCALARS] * 3 + [RESIDENT] * (3 + len(others)),
        out_specs=[RESIDENT] * 2,
        out_shape=[
            pltpu.VMEM(grads.shape, jnp.float32),
            pltpu.VMEM(loss.shape, jnp.float32),
        ],
        scratch_shapes=score_scratch(count),
        input_output_aliases={at: 0, at + 1: 1},
        compiler_params=pltpu.CompilerParams(vmem_limit_bytes=VMEM_LIMIT),
        cost_estimate=NO_COST,
        name="add_pairs",
    )(*scalars, *map(kept, others), kept(emb), kept(grads), kept(loss))


def finish_pairs(side, scalars, other, emb, grads, loss, images, texts, outs=()):
    count = other.shape[0]
    last = side == FAR
    return pl.pallas_call(
        functools.partial(finish_kernel, side=side),
        in_specs=[SCALARS] * 3 + [RESIDENT] * 4 + [ANYWHERE] * (2 + len(outs)),
        out_specs=[RESIDENT, ANYWHERE, ANYWHERE],
        out_shape=[
            jax.ShapeDtypeStruct((RB,), jnp.float32)
            if last
            else pltpu.VMEM(loss.shape, jnp.float32),
            jax.ShapeDtypeStruct((RB, D), jnp.float32),
            jax.ShapeDtypeStruct((RB, D), jnp.float32),
        ],
        scratch_shapes=score_scratch(count)
        + [
            pltpu.VMEM((RB, D), jnp.bfloat16),
            pltpu.VMEM((RB, D), jnp.float32),
            pltpu.SemaphoreType.DMA,
            pltpu.SemaphoreType.DMA((PARTS,)),
        ]
        + ([pltpu.VMEM(loss.shape, jnp.float32)] if last else []),
        input_output_aliases={9: 1, 10: 2} if last else {6: 0},
        compiler_params=pltpu.CompilerParams(vmem_limit_bytes=VMEM_LIMIT),
        cost_estimate=NO_COST,
        name="finish_pairs",
    )(
        *scalars,
        kept(other),
        kept(emb),
        kept(grads),
        kept(loss),
        in_hbm(images),
        in_hbm(texts),
        *outs,
    )


def per_device(images, texts, log_scale, logit_bias):
    count = lax.axis_size("blk")
    odd = (lax.axis_index("blk") % 2).astype(jnp.int32)[None]
    scalars = (odd, log_scale, logit_bias)

    first = [(i, (i + 2) % count if i % 2 else (i - 2) % count) for i in range(count)]
    second = [(i, (i + 1) % count if i % 2 else (i - 1) % count) for i in range(count)]
    across = [(i, i ^ 1) for i in range(count)]

    def send(block, pairs):
        return lax.ppermute(block, "blk", pairs)

    far = pick(odd, images, texts)
    far_other = send(far, first)
    emb, near_head, near_tail = prepare(odd, images, texts, far)
    beside_head = send(near_head, across)
    beside_tail = send(near_tail, across)
    beside_head, beside_tail, emb = lax.optimization_barrier((beside_head, beside_tail, emb))
    near_head_other = send(beside_head, second)
    grads, loss = own_pairs(*scalars, emb)
    beside_tail, grads = lax.optimization_barrier((beside_tail, grads))
    near_tail_other = send(beside_tail, second)
    grads, loss = add_pairs(NEAR, scalars, [beside_head, beside_tail], emb, grads, loss)
    far_other, grads = lax.optimization_barrier((far_other, grads))
    far_beside = [send(far_other[at : at + PIECE], across) for at in range(0, RB, PIECE)]
    loss, *outs = finish_pairs(NEAR, scalars, far_other, emb, grads, loss, images, texts)
    grads, loss = add_pairs(FAR, scalars, far_beside, emb, grads, loss)
    grads, loss = add_pairs(FAR, scalars, [near_head_other], emb, grads, loss)
    row_loss, image_grad, text_grad = finish_pairs(
        FAR, scalars, near_tail_other, emb, grads, loss, images, texts, outs
    )
    return (row_loss, image_grad, text_grad)


def solution(mesh):
    placed = (P("blk", None), P("blk", None), P(), P())
    return jax.shard_map(
        per_device,
        mesh=mesh,
        in_specs=placed,
        out_specs=(P("blk"), P("blk", None), P("blk", None)),
        check_vma=False,
    )
```

time: 63.5 us -> 58.2 us (0.917)
  the two profiles are of different devices: /device:TPU:0 before, /device:TPU:1 now
where the time goes in v3:
time: 58.2 us; the launch traced here: 58 us
  Pallas kernels  33.1 us (57%)
  starting transfers between devices  19 us (33%)
  waiting for transfers between devices  3.65 us (6%)
  between operations  2.22 us (4%)
    ppermute x8, starting transfers between devices, send(): return lax.ppermute(block, 'blk', pairs)  19 us
    pallas_call x2, Pallas kernels, finish_pairs(): pl.pallas_call(functools.partial(finish_kernel, side=side), in_specs=[SCA...  12.2 us
    pallas_call x3, Pallas kernels, add_pairs(): pl.pallas_call(functools.partial(add_kernel, side=side, pieces=len(others...  11.8 us
    pallas_call x1, Pallas kernels, own_pairs(): pl.pallas_call(own_kernel, in_specs=[SCALARS] * 3 + [RESIDENT], out_specs...  5.59 us
    ppermute x8, waiting for transfers between devices, send(): return lax.ppermute(block, 'blk', pairs)  3.65 us
    pallas_call x1, Pallas kernels, prepare(): pl.pallas_call(prepare_kernel, in_specs=[SCALARS, ANYWHERE, ANYWHERE, RES...  2 us
    pallas_call x1, Pallas kernels, pick(): pl.pallas_call(pick_kernel, in_specs=[SCALARS, ANYWHERE, ANYWHERE], out_s...  1.49 us
  transfers between devices with their start and end apart: 8, of which 2 were waited for; matrix products, arithmetic and copies ran while one was open for 0% of the time, Pallas kernels for 45%

profile of v3, /device:TPU:1, one launch (start us, length us, event | category | flops | bytes accessed | tf_op | source)
XLA Modules:
  0.0 58.0 jit_solution(4419819544385827381)
XLA Ops:
  0.6 1.5 %pick.1.far = bf16[768,1152]{1,0:T(8,128)(2,1)S(1)} custom-call(s32[1]{0:T(128)} %bitcast.odd.refs_0_, bf16[768,1152]{1,0:T(8,128)(2,1)} %refs_7_.3, bf16[768,1152]{1,0:T(8,128)(2,1)} %refs_8_.3), custom_call_target="tpu_custom_call" | custom-call | flops 1 | bytes 1 | tf_op jit(solution)/shard_map/pick/pallas_call | solution.py:83
  2.1 2.1 %collective-permute-start.4 = (bf16[768,1152]{1,0:T(8,128)(2,1)S(1)}, bf16[768,1152]{1,0:T(8,128)(2,1)S(1)}, u32[]{:S(2)}, u32[]{:S(2)}) collective-permute-start(bf16[768,1152]{1,0:T(8,128)(2,1)S(1)} %pick.1.far), channel_id=1, source_target_pairs={{0,254},{1,3},{2,0},{3,5},{4,2},{5,7},{6,4},{7,9},{8,6},{9,11},{10... | collective-permute-start | bytes 5308424 | tf_op jit(solution)/shard_map/ppermute | solution.py:344
  4.3 2.0 %prepare.1 = (bf16[2,768,1152]{2,1,0:T(8,128)(2,1)S(1)}, bf16[400,1152]{1,0:T(8,128)(2,1)S(1)}, bf16[368,1152]{1,0:T(8,128)(2,1)S(1)}) custom-call(s32[1]{0:T(128)} %bitcast.odd.refs_0_, bf16[768,1152]{1,0:T(8,128)(2,1)} %refs_7_.3, bf16[768,1152]{1,0:T(8,128)(2,1)} %refs_8_.3, bf16[768,1152]{1,0:T(8,128)(2,1)S(1)} %pick.1.far), custom_call_target="tpu_custom_call" | custom-call | flops 1 | bytes 1 | tf_op jit(solution)/shard_map/prepare/pallas_call | solution.py:113
  6.3 10.1 %collective-permute-start = (bf16[400,1152]{1,0:T(8,128)(2,1)S(1)}, bf16[400,1152]{1,0:T(8,128)(2,1)S(1)}, u32[]{:S(2)}, u32[]{:S(2)}) collective-permute-start(bf16[400,1152]{1,0:T(8,128)(2,1)S(1)} %get-tuple-element.24), channel_id=1, source_target_pairs={{0,1},{1,0},{2,3},{3,2},{4,5},{5,4},{6,7},{7,6},{8,9},{9,8},{10,11... | collective-permute-start | bytes 2764808 | tf_op jit(solution)/shard_map/ppermute | solution.py:344
  16.3 0.1 collective-permute-start.1
  17.7 1.9 %collective-permute-done.1.refs_4_ = bf16[368,1152]{1,0:T(8,128)(2,1)S(1)} collective-permute-done((bf16[368,1152]{1,0:T(8,128)(2,1)S(1)}, bf16[368,1152]{1,0:T(8,128)(2,1)S(1)}, u32[]{:S(2)}, u32[]{:S(2)}) %collective-permute-start.1) | collective-permute-done | bytes 847904 | tf_op jit(solution)/shard_map/ppermute | solution.py:344
  19.6 0.0 collective-permute-done.refs_3_
  19.6 0.0 collective-permute-start.3
  19.6 5.6 %own_pairs.1 = (f32[2,768,1152]{2,1,0:T(8,128)S(1)}, f32[768,128]{1,0:T(8,128)S(1)}) custom-call(s32[1]{0:T(128)} %bitcast.odd.refs_0_, f32[1]{0:T(128)S(6)} %copy.25.log_scale.refs_1_, f32[1]{0:T(128)S(6)} %copy.26.logit_bias.refs_2_, bf16[2,768,1152]{2,1,0:T(8,128)(2,1)S(1)} %get-tuple-element.28.emb.refs_5_.refs_4_.refs_6_), custom_call_target="tpu_custom_call" | custom-call | flops 1 | bytes 1 | tf_op jit(solution)/shard_map/own_pairs/pallas_call | solution.py:158
  25.2 2.0 %collective-permute-start.2 = (bf16[368,1152]{1,0:T(8,128)(2,1)S(1)}, bf16[368,1152]{1,0:T(8,128)(2,1)S(1)}, u32[]{:S(2)}, u32[]{:S(2)}) collective-permute-start(bf16[368,1152]{1,0:T(8,128)(2,1)S(1)} %collective-permute-done.1.refs_4_), channel_id=1, source_target_pairs={{0,255},{1,2},{2,1},{3,4},{4,3},{5,6},{6,5},{7,8},{8,7},{9,10},{10... | collective-permute-start | bytes 2543624 | tf_op jit(solution)/shard_map/ppermute | solution.py:344
  27.2 4.2 %add_pairs.3 = (f32[2,768,1152]{2,1,0:T(8,128)S(1)}, f32[768,128]{1,0:T(8,128)S(1)}) custom-call(s32[1]{0:T(128)} %bitcast.odd.refs_0_, f32[1]{0:T(128)S(6)} %copy.25.log_scale.refs_1_, f32[1]{0:T(128)S(6)} %copy.26.logit_bias.refs_2_, bf16[400,1152]{1,0:T(8,128)(2,1)S(1)} %collective-permute-done.refs_3_, ...), custom_call_target="tpu_custom_call", output_to_operand_aliasing={{0}: (6, {}), {1}: (7, {})} | custom-call | flops 1 | bytes 1 | tf_op jit(solution)/shard_map/add_pairs/pallas_call | solution.py:280
  31.5 1.7 %collective-permute-done.4.refs_3_ = bf16[768,1152]{1,0:T(8,128)(2,1)S(1)} collective-permute-done((bf16[768,1152]{1,0:T(8,128)(2,1)S(1)}, bf16[768,1152]{1,0:T(8,128)(2,1)S(1)}, u32[]{:S(2)}, u32[]{:S(2)}) %collective-permute-start.4) | collective-permute-done | bytes 1769504 | tf_op jit(solution)/shard_map/ppermute | solution.py:344
  33.2 0.1 fusion
  33.3 4.2 %collective-permute-start.7 = (bf16[256,1152]{1,0:T(8,128)(2,1)S(1)}, bf16[256,1152]{1,0:T(8,128)(2,1)S(1)}, u32[]{:S(2)}, u32[]{:S(2)}) collective-permute-start(bf16[256,1152]{1,0:T(8,128)(2,1)S(1)} %get-tuple-element.45), channel_id=1, source_target_pairs={{0,1},{1,0},{2,3},{3,2},{4,5},{5,4},{6,7},{7,6},{8,9},{9,8},{10,11... | collective-permute-start | bytes 1769480 | tf_op jit(solution)/shard_map/ppermute | solution.py:344
  37.5 0.1 collective-permute-start.6
  37.6 0.4 collective-permute-start.5
  38.0 6.6 %finish_pairs.2 = (f32[768,128]{1,0:T(8,128)S(1)}, f32[768,1152]{1,0:T(8,128)}, f32[768,1152]{1,0:T(8,128)}) custom-call(s32[1]{0:T(128)} %bitcast.odd.refs_0_, f32[1]{0:T(128)S(6)} %copy.25.log_scale.refs_1_, f32[1]{0:T(128)S(6)} %copy.26.logit_bias.refs_2_, bf16[768,1152]{1,0:T(8,128)(2,1)S(1)} %collective-permute-done.4.refs_3_, ...), custom_call_target="tpu_custom_call", output_to_operand_aliasing={{0}: (6, {})} | custom-call | flops 1 | bytes 1 | tf_op jit(solution)/shard_map/finish_pairs/pallas_call | solution.py:299
  44.7 0.0 collective-permute-done.7.refs_5_
  44.7 0.0 collective-permute-done.6.refs_4_
  44.7 0.0 collective-permute-done.5.refs_3_
  44.7 4.2 %add_pairs.4 = (f32[2,768,1152]{2,1,0:T(8,128)S(1)}, f32[768,128]{1,0:T(8,128)S(1)}) custom-call(s32[1]{0:T(128)} %bitcast.odd.refs_0_, f32[1]{0:T(128)S(6)} %copy.25.log_scale.refs_1_, f32[1]{0:T(128)S(6)} %copy.26.logit_bias.refs_2_, bf16[256,1152]{1,0:T(8,128)(2,1)S(1)} %collective-permute-done.5.refs_3_, ...), custom_call_target="tpu_custom_call", output_to_operand_aliasing={{0}: (7, {}), {1}: (8, {})} | custom-call | flops 1 | bytes 1 | tf_op jit(solution)/shard_map/add_pairs/pallas_call | solution.py:280
  48.9 0.0 collective-permute-done.3.refs_3_
  48.9 3.4 %add_pairs.5 = (f32[2,768,1152]{2,1,0:T(8,128)S(1)}, f32[768,128]{1,0:T(8,128)S(1)}) custom-call(s32[1]{0:T(128)} %bitcast.odd.refs_0_, f32[1]{0:T(128)S(6)} %copy.25.log_scale.refs_1_, f32[1]{0:T(128)S(6)} %copy.26.logit_bias.refs_2_, bf16[400,1152]{1,0:T(8,128)(2,1)S(1)} %collective-permute-done.3.refs_3_, ...), custom_call_target="tpu_custom_call", output_to_operand_aliasing={{0}: (5, {}), {1}: (6, {})} | custom-call | flops 1 | bytes 1 | tf_op jit(solution)/shard_map/add_pairs/pallas_call | solution.py:280
  52.3 5.5 %finish_pairs.3 = (f32[768]{0:T(1024)}, f32[768,1152]{1,0:T(8,128)}, f32[768,1152]{1,0:T(8,128)}) custom-call(s32[1]{0:T(128)} %bitcast.odd.refs_0_, f32[1]{0:T(128)S(6)} %copy.25.log_scale.refs_1_, f32[1]{0:T(128)S(6)} %copy.26.logit_bias.refs_2_, ...), custom_call_target="tpu_custom_call", output_to_operand_aliasing={{1}: (9, {}), {2}: (10, {})} | custom-call | flops 1 | bytes 1 | tf_op jit(solution)/shard_map/finish_pairs/pallas_call | solution.py:299
  (1 shorter events, 0.0 us)
Async XLA Ops:
  2.1 31.0 %collective-permute-start.4 = (bf16[768,1152]{1,0:T(8,128)(2,1)S(1)}, bf16[768,1152]{1,0:T(8,128)(2,1)S(1)}, u32[]{:S(2)}, u32[]{:S(2)}) collective-permute-start(bf16[768,1152]{1,0:T(8,128)(2,1)S(1)} %pick.1.far), channel_id=1, source_target_pairs={{0,254},{1,3},{2,0},{3,5},{4,2},{5,7},{6,4},{7,9},{8,6},{9,11},{10... | collective-permute-start | bytes 5308424 | tf_op jit(solution)/shard_map/ppermute | solution.py:344
  6.3 13.4 %collective-permute-start = (bf16[400,1152]{1,0:T(8,128)(2,1)S(1)}, bf16[400,1152]{1,0:T(8,128)(2,1)S(1)}, u32[]{:S(2)}, u32[]{:S(2)}) collective-permute-start(bf16[400,1152]{1,0:T(8,128)(2,1)S(1)} %get-tuple-element.24), channel_id=1, source_target_pairs={{0,1},{1,0},{2,3},{3,2},{4,5},{5,4},{6,7},{7,6},{8,9},{9,8},{10,11... | collective-permute-start | bytes 2764808 | tf_op jit(solution)/shard_map/ppermute | solution.py:344
  16.3 3.3 %collective-permute-start.1 = (bf16[368,1152]{1,0:T(8,128)(2,1)S(1)}, bf16[368,1152]{1,0:T(8,128)(2,1)S(1)}, u32[]{:S(2)}, u32[]{:S(2)}) collective-permute-start(bf16[368,1152]{1,0:T(8,128)(2,1)S(1)} %get-tuple-element.25), channel_id=1, source_target_pairs={{0,1},{1,0},{2,3},{3,2},{4,5},{5,4},{6,7},{7,6},{8,9},{9,8},{10,11... | collective-permute-start | bytes 2543624 | tf_op jit(solution)/shard_map/ppermute | solution.py:344
  19.6 29.3 %collective-permute-start.3 = (bf16[400,1152]{1,0:T(8,128)(2,1)S(1)}, bf16[400,1152]{1,0:T(8,128)(2,1)S(1)}, u32[]{:S(2)}, u32[]{:S(2)}) collective-permute-start(bf16[400,1152]{1,0:T(8,128)(2,1)S(1)} %collective-permute-done.refs_3_), channel_id=1, source_target_pairs={{0,255},{1,2},{2,1},{3,4},{4,3},{5,6},{6,5},{7,8},{8,7},{9,10},{10... | collective-permute-start | bytes 2764808 | tf_op jit(solution)/shard_map/ppermute | solution.py:344
  25.2 27.1 %collective-permute-start.2 = (bf16[368,1152]{1,0:T(8,128)(2,1)S(1)}, bf16[368,1152]{1,0:T(8,128)(2,1)S(1)}, u32[]{:S(2)}, u32[]{:S(2)}) collective-permute-start(bf16[368,1152]{1,0:T(8,128)(2,1)S(1)} %collective-permute-done.1.refs_4_), channel_id=1, source_target_pairs={{0,255},{1,2},{2,1},{3,4},{4,3},{5,6},{6,5},{7,8},{8,7},{9,10},{10... | collective-permute-start | bytes 2543624 | tf_op jit(solution)/shard_map/ppermute | solution.py:344
  33.3 11.3 %collective-permute-start.7 = (bf16[256,1152]{1,0:T(8,128)(2,1)S(1)}, bf16[256,1152]{1,0:T(8,128)(2,1)S(1)}, u32[]{:S(2)}, u32[]{:S(2)}) collective-permute-start(bf16[256,1152]{1,0:T(8,128)(2,1)S(1)} %get-tuple-element.45), channel_id=1, source_target_pairs={{0,1},{1,0},{2,3},{3,2},{4,5},{5,4},{6,7},{7,6},{8,9},{9,8},{10,11... | collective-permute-start | bytes 1769480 | tf_op jit(solution)/shard_map/ppermute | solution.py:344
  37.5 7.2 %collective-permute-start.6 = (bf16[256,1152]{1,0:T(8,128)(2,1)S(1)}, bf16[256,1152]{1,0:T(8,128)(2,1)S(1)}, u32[]{:S(2)}, u32[]{:S(2)}) collective-permute-start(bf16[256,1152]{1,0:T(8,128)(2,1)S(1)} %get-tuple-element.46), channel_id=1, source_target_pairs={{0,1},{1,0},{2,3},{3,2},{4,5},{5,4},{6,7},{7,6},{8,9},{9,8},{10,11... | collective-permute-start | bytes 1769480 | tf_op jit(solution)/shard_map/ppermute | solution.py:344
  37.6 7.1 %collective-permute-start.5 = (bf16[256,1152]{1,0:T(8,128)(2,1)S(1)}, bf16[256,1152]{1,0:T(8,128)(2,1)S(1)}, u32[]{:S(2)}, u32[]{:S(2)}) collective-permute-start(bf16[256,1152]{1,0:T(8,128)(2,1)S(1)} %get-tuple-element.47), channel_id=1, source_target_pairs={{0,1},{1,0},{2,3},{3,2},{4,5},{5,4},{6,7},{7,6},{8,9},{9,8},{10,11... | collective-permute-start | bytes 1769480 | tf_op jit(solution)/shard_map/ppermute | solution.py:344

commit v4 on v3

--- a/solution.py
+++ b/solution.py
@@ -14,7 +14,7 @@
 TILE = 256
 LANES = 128
 PARTS = RB // TILE
-VMEM_LIMIT = 12 * 1024 * 1024
+VMEM_LIMIT = 16 * 1024 * 1024
 CUT = 400
 PIECE = 256
 NEAR, FAR = 0, 1
@@ -189,7 +189,7 @@
 
 def score(side, has_loss, log_scale, logit_bias, emb, loss_in, loss, other_emb, slopes, valid):
     count = other_emb.shape[0]
-    step = RB if count == RB else TILE
+    step = RB if count >= RB else TILE
     for row in range(0, RB, step):
         rows = slice(row, row + step)
         losses = jnp.zeros((step, LANES), jnp.float32)
@@ -210,32 +210,38 @@
         loss[rows] = loss_in[rows] + jnp.where(has_loss, losses, 0.0)
 
 
-def add_kernel(*refs, side, pieces):
+def add_kernel(*refs, side, pieces, fetch):
     odd, log_scale, logit_bias, *others = refs[: 3 + pieces]
-    emb, grads_in, loss_in, grads, loss, other_emb, slopes = refs[3 + pieces :]
+    emb, grads_in, loss_in, *refs = refs[3 + pieces :]
+    has_loss = odd[0] == (1 if side == NEAR else 0)
+    if fetch:
+        images, texts, grads, loss, raw, other_emb, slopes, raw_sem = refs
+        copy_if(has_loss, images, raw, raw_sem)
+        copy_if(jnp.logical_not(has_loss), texts, raw, raw_sem)
+    else:
+        grads, loss, other_emb, slopes = refs
     valid = embed_all(others, other_emb)
-    has_loss = odd[0] == (1 if side == NEAR else 0)
     score(side, has_loss, log_scale, logit_bias, emb, loss_in, loss, other_emb, slopes, valid)
     scale_wide = scale_row(log_scale, D)
-    step = RB if other_emb.shape[0] == RB else TILE
+    step = RB if other_emb.shape[0] >= RB else TILE
     for row in range(0, RB, step):
         rows = slice(row, row + step)
         grads[side, rows] = grads_in[side, rows] + scale_wide * matmul(
             slopes[rows], other_emb[...]
         )
+    if fetch:
+        pltpu.make_async_copy(images, raw, raw_sem).wait()
 
 
 def finish_kernel(*refs, side):
-    odd, log_scale, logit_bias, other, emb, grads, loss_in, images, texts = refs[:9]
+    odd, log_scale, logit_bias, other, emb, grads, loss_in, raw = refs[:8]
     if side == FAR:
         refs = refs[2:]
-    loss, image_grad, text_grad, *scratch = refs[9:]
-    other_emb, slopes, raw, finished, raw_sem, out_sems = scratch[:6]
+    loss, image_grad, text_grad, *scratch = refs[8:]
+    other_emb, slopes, finished, out_sems = scratch[:4]
     of_images = odd[0] == (1 if side == NEAR else 0)
-    copy_if(of_images, images, raw, raw_sem)
-    copy_if(jnp.logical_not(of_images), texts, raw, raw_sem)
     valid = embed_all([other], other_emb)
-    sums = loss if side == NEAR else scratch[6]
+    sums = loss if side == NEAR else scratch[4]
     score(side, of_images, log_scale, logit_bias, emb, loss_in, sums, other_emb, slopes, valid)
     scale_wide = scale_row(log_scale, D)
 
@@ -249,7 +255,6 @@
 
     if side == NEAR:
         accumulate(slice(0, RB))
-    pltpu.make_async_copy(images, raw, raw_sem).wait()
     for row in range(PARTS):
         here = tile(row)
         if side == FAR:
@@ -274,31 +279,40 @@
     ]
 
 
-def add_pairs(side, scalars, others, emb, grads, loss):
+def add_pairs(side, scalars, others, emb, grads, loss, fetch=()):
     count = sum(other.shape[0] for other in others)
     at = 4 + len(others)
-    return pl.pallas_call(
-        functools.partial(add_kernel, side=side, pieces=len(others)),
-        in_specs=[SCALARS] * 3 + [RESIDENT] * (3 + len(others)),
-        out_specs=[RESIDENT] * 2,
+    raw = pltpu.VMEM((RB, D), jnp.bfloat16)
+    return pl.pallas_call(
+        functools.partial(add_kernel, side=side, pieces=len(others), fetch=bool(fetch)),
+        in_specs=[SCALARS] * 3 + [RESIDENT] * (3 + len(others)) + [ANYWHERE] * len(fetch),
+        out_specs=[RESIDENT] * (3 if fetch else 2),
         out_shape=[
             pltpu.VMEM(grads.shape, jnp.float32),
             pltpu.VMEM(loss.shape, jnp.float32),
-        ],
-        scratch_shapes=score_scratch(count),
+        ]
+        + ([raw] if fetch else []),
+        scratch_shapes=score_scratch(count) + ([pltpu.SemaphoreType.DMA] if fetch else []),
         input_output_aliases={at: 0, at + 1: 1},
         compiler_params=pltpu.CompilerParams(vmem_limit_bytes=VMEM_LIMIT),
         cost_estimate=NO_COST,
         name="add_pairs",
-    )(*scalars, *map(kept, others), kept(emb), kept(grads), kept(loss))
-
-
-def finish_pairs(side, scalars, other, emb, grads, loss, images, texts, outs=()):
+    )(
+        *scalars,
+        *map(kept, others),
+        kept(emb),
+        kept(grads),
+        kept(loss),
+        *map(in_hbm, fetch),
+    )
+
+
+def finish_pairs(side, scalars, other, emb, grads, loss, raw, outs=()):
     count = other.shape[0]
     last = side == FAR
     return pl.pallas_call(
         functools.partial(finish_kernel, side=side),
-        in_specs=[SCALARS] * 3 + [RESIDENT] * 4 + [ANYWHERE] * (2 + len(outs)),
+        in_specs=[SCALARS] * 3 + [RESIDENT] * 5 + [ANYWHERE] * len(outs),
         out_specs=[RESIDENT, ANYWHERE, ANYWHERE],
         out_shape=[
             jax.ShapeDtypeStruct((RB,), jnp.float32)
@@ -309,13 +323,11 @@
         ],
         scratch_shapes=score_scratch(count)
         + [
-            pltpu.VMEM((RB, D), jnp.bfloat16),
             pltpu.VMEM((RB, D), jnp.float32),
-            pltpu.SemaphoreType.DMA,
             pltpu.SemaphoreType.DMA((PARTS,)),
         ]
         + ([pltpu.VMEM(loss.shape, jnp.float32)] if last else []),
-        input_output_aliases={9: 1, 10: 2} if last else {6: 0},
+        input_output_aliases={8: 1, 9: 2} if last else {6: 0},
         compiler_params=pltpu.CompilerParams(vmem_limit_bytes=VMEM_LIMIT),
         cost_estimate=NO_COST,
         name="finish_pairs",
@@ -325,8 +337,7 @@
         kept(emb),
         kept(grads),
         kept(loss),
-        in_hbm(images),
-        in_hbm(texts),
+        kept(raw),
         *outs,
     )
 
@@ -353,14 +364,17 @@
     grads, loss = own_pairs(*scalars, emb)
     beside_tail, grads = lax.optimization_barrier((beside_tail, grads))
     near_tail_other = send(beside_tail, second)
-    grads, loss = add_pairs(NEAR, scalars, [beside_head, beside_tail], emb, grads, loss)
+    grads, loss, raw = add_pairs(
+        NEAR, scalars, [beside_head, beside_tail], emb, grads, loss, (images, texts)
+    )
     far_other, grads = lax.optimization_barrier((far_other, grads))
     far_beside = [send(far_other[at : at + PIECE], across) for at in range(0, RB, PIECE)]
-    loss, *outs = finish_pairs(NEAR, scalars, far_other, emb, grads, loss, images, texts)
-    grads, loss = add_pairs(FAR, scalars, far_beside, emb, grads, loss)
-    grads, loss = add_pairs(FAR, scalars, [near_head_other], emb, grads, loss)
+    loss, *outs = finish_pairs(NEAR, scalars, far_other, emb, grads, loss, raw)
+    grads, loss, raw = add_pairs(
+        FAR, scalars, [*far_beside, near_head_other], emb, grads, loss, (images, texts)
+    )
     row_loss, image_grad, text_grad = finish_pairs(
-        FAR, scalars, near_tail_other, emb, grads, loss, images, texts, outs
+        FAR, scalars, near_tail_other, emb, grads, loss, raw, outs
     )
     return (row_loss, image_grad, text_grad)
 

time: 58.2 us -> 56.7 us (0.974)
  Pallas kernels: 33.1 us -> 31.6 us
    pallas_call x3 -> x2, Pallas kernels: 11.8 us -> 10.7 us  [add_pairs(): pl.pallas_call(functools.partial(add_kernel, side=side, pieces=len(others...]
  transfers between devices with their start and end apart: 8 -> 8, of which waited for: 2 -> 2; matrix products, arithmetic and copies ran while one was open for 0% -> 0% of each run, Pallas kernels for 45% -> 44%
where the time goes in v4:
time: 56.7 us; the launch traced here: 56.6 us
  Pallas kernels  31.6 us (56%)
  starting transfers between devices  19 us (34%)
  waiting for transfers between devices  3.68 us (6%)
  between operations  2.19 us (4%)
    ppermute x8, starting transfers between devices, send(): return lax.ppermute(block, 'blk', pairs)  19 us
    pallas_call x2, Pallas kernels, finish_pairs(): pl.pallas_call(functools.partial(finish_kernel, side=side), in_specs=[SCA...  11.8 us
    pallas_call x2, Pallas kernels, add_pairs(): pl.pallas_call(functools.partial(add_kernel, side=side, pieces=len(others...  10.7 us
    pallas_call x1, Pallas kernels, own_pairs(): pl.pallas_call(own_kernel, in_specs=[SCALARS] * 3 + [RESIDENT], out_specs...  5.59 us
    ppermute x8, waiting for transfers between devices, send(): return lax.ppermute(block, 'blk', pairs)  3.68 us
    pallas_call x1, Pallas kernels, prepare(): pl.pallas_call(prepare_kernel, in_specs=[SCALARS, ANYWHERE, ANYWHERE, RES...  2 us
    pallas_call x1, Pallas kernels, pick(): pl.pallas_call(pick_kernel, in_specs=[SCALARS, ANYWHERE, ANYWHERE], out_s...  1.49 us
  transfers between devices with their start and end apart: 8, of which 2 were waited for; matrix products, arithmetic and copies ran while one was open for 0% of the time, Pallas kernels for 44%

profile of v4, /device:TPU:1, one launch (start us, length us, event | category | flops | bytes accessed | tf_op | source)
XLA Modules:
  0.0 56.6 jit_solution(15060410979919114984)
XLA Ops:
  0.6 1.5 %pick.1.far = bf16[768,1152]{1,0:T(8,128)(2,1)S(1)} custom-call(s32[1]{0:T(128)} %bitcast.odd.refs_0_, bf16[768,1152]{1,0:T(8,128)(2,1)} %refs_10_.1, bf16[768,1152]{1,0:T(8,128)(2,1)} %refs_11_.1), custom_call_target="tpu_custom_call" | custom-call | flops 1 | bytes 1 | tf_op jit(solution)/shard_map/pick/pallas_call | solution.py:83
  2.1 2.1 %collective-permute-start.3 = (bf16[768,1152]{1,0:T(8,128)(2,1)S(1)}, bf16[768,1152]{1,0:T(8,128)(2,1)S(1)}, u32[]{:S(2)}, u32[]{:S(2)}) collective-permute-start(bf16[768,1152]{1,0:T(8,128)(2,1)S(1)} %pick.1.far), channel_id=1, source_target_pairs={{0,254},{1,3},{2,0},{3,5},{4,2},{5,7},{6,4},{7,9},{8,6},{9,11},{10... | collective-permute-start | bytes 5308424 | tf_op jit(solution)/shard_map/ppermute | solution.py:355
  4.3 2.0 %prepare.1 = (bf16[2,768,1152]{2,1,0:T(8,128)(2,1)S(1)}, bf16[400,1152]{1,0:T(8,128)(2,1)S(1)}, bf16[368,1152]{1,0:T(8,128)(2,1)S(1)}) custom-call(s32[1]{0:T(128)} %bitcast.odd.refs_0_, bf16[768,1152]{1,0:T(8,128)(2,1)} %refs_10_.1, bf16[768,1152]{1,0:T(8,128)(2,1)} %refs_11_.1, bf16[768,1152]{1,0:T(8,128)(2,1)S(1)} %pick.1.far), custom_call_target="tpu_custom_call" | custom-call | flops 1 | bytes 1 | tf_op jit(solution)/shard_map/prepare/pallas_call | solution.py:113
  6.3 10.1 %collective-permute-start = (bf16[400,1152]{1,0:T(8,128)(2,1)S(1)}, bf16[400,1152]{1,0:T(8,128)(2,1)S(1)}, u32[]{:S(2)}, u32[]{:S(2)}) collective-permute-start(bf16[400,1152]{1,0:T(8,128)(2,1)S(1)} %get-tuple-element.24), channel_id=1, source_target_pairs={{0,1},{1,0},{2,3},{3,2},{4,5},{5,4},{6,7},{7,6},{8,9},{9,8},{10,11... | collective-permute-start | bytes 2764808 | tf_op jit(solution)/shard_map/ppermute | solution.py:355
  16.3 0.1 collective-permute-start.1
  17.7 1.9 %collective-permute-done.1.refs_4_ = bf16[368,1152]{1,0:T(8,128)(2,1)S(1)} collective-permute-done((bf16[368,1152]{1,0:T(8,128)(2,1)S(1)}, bf16[368,1152]{1,0:T(8,128)(2,1)S(1)}, u32[]{:S(2)}, u32[]{:S(2)}) %collective-permute-start.1) | collective-permute-done | bytes 847904 | tf_op jit(solution)/shard_map/ppermute | solution.py:355
  19.6 0.0 collective-permute-done.refs_3_
  19.6 0.0 collective-permute-start.7
  19.6 5.6 %own_pairs.1 = (f32[2,768,1152]{2,1,0:T(8,128)S(1)}, f32[768,128]{1,0:T(8,128)S(1)}) custom-call(s32[1]{0:T(128)} %bitcast.odd.refs_0_, f32[1]{0:T(128)S(6)} %copy.21.log_scale.refs_1_, f32[1]{0:T(128)S(6)} %copy.22.logit_bias.refs_2_, bf16[2,768,1152]{2,1,0:T(8,128)(2,1)S(1)} %get-tuple-element.28.emb.refs_5_.refs_4_.refs_7_), custom_call_target="tpu_custom_call" | custom-call | flops 1 | bytes 1 | tf_op jit(solution)/shard_map/own_pairs/pallas_call | solution.py:158
  25.2 2.0 %collective-permute-start.2 = (bf16[368,1152]{1,0:T(8,128)(2,1)S(1)}, bf16[368,1152]{1,0:T(8,128)(2,1)S(1)}, u32[]{:S(2)}, u32[]{:S(2)}) collective-permute-start(bf16[368,1152]{1,0:T(8,128)(2,1)S(1)} %collective-permute-done.1.refs_4_), channel_id=1, source_target_pairs={{0,255},{1,2},{2,1},{3,4},{4,3},{5,6},{6,5},{7,8},{8,7},{9,10},{10... | collective-permute-start | bytes 2543624 | tf_op jit(solution)/shard_map/ppermute | solution.py:355
  27.2 4.2 %add_pairs.2 = (f32[2,768,1152]{2,1,0:T(8,128)S(1)}, f32[768,128]{1,0:T(8,128)S(1)}, bf16[768,1152]{1,0:T(8,128)(2,1)S(1)}) custom-call(s32[1]{0:T(128)} %bitcast.odd.refs_0_, f32[1]{0:T(128)S(6)} %copy.21.log_scale.refs_1_, f32[1]{0:T(128)S(6)} %copy.22.logit_bias.refs_2_, ...), custom_call_target="tpu_custom_call", output_to_operand_aliasing={{0}: (6, {}), {1}: (7, {})} | custom-call | flops 1 | bytes 1 | tf_op jit(solution)/shard_map/add_pairs/pallas_call | solution.py:286
  31.4 1.7 %collective-permute-done.3.refs_3_ = bf16[768,1152]{1,0:T(8,128)(2,1)S(1)} collective-permute-done((bf16[768,1152]{1,0:T(8,128)(2,1)S(1)}, bf16[768,1152]{1,0:T(8,128)(2,1)S(1)}, u32[]{:S(2)}, u32[]{:S(2)}) %collective-permute-start.3) | collective-permute-done | bytes 1769504 | tf_op jit(solution)/shard_map/ppermute | solution.py:355
  33.2 0.1 fusion
  33.3 4.2 %collective-permute-start.6 = (bf16[256,1152]{1,0:T(8,128)(2,1)S(1)}, bf16[256,1152]{1,0:T(8,128)(2,1)S(1)}, u32[]{:S(2)}, u32[]{:S(2)}) collective-permute-start(bf16[256,1152]{1,0:T(8,128)(2,1)S(1)} %get-tuple-element.45), channel_id=1, source_target_pairs={{0,1},{1,0},{2,3},{3,2},{4,5},{5,4},{6,7},{7,6},{8,9},{9,8},{10,11... | collective-permute-start | bytes 1769480 | tf_op jit(solution)/shard_map/ppermute | solution.py:355
  37.5 0.1 collective-permute-start.5
  37.6 0.4 collective-permute-start.4
  38.0 6.6 %finish_pairs.2 = (f32[768,128]{1,0:T(8,128)S(1)}, f32[768,1152]{1,0:T(8,128)}, f32[768,1152]{1,0:T(8,128)}) custom-call(s32[1]{0:T(128)} %bitcast.odd.refs_0_, f32[1]{0:T(128)S(6)} %copy.21.log_scale.refs_1_, f32[1]{0:T(128)S(6)} %copy.22.logit_bias.refs_2_, bf16[768,1152]{1,0:T(8,128)(2,1)S(1)} %collective-permute-done.3.refs_3_, ...), custom_call_target="tpu_custom_call", output_to_operand_aliasing={{0}: (6, {})} | custom-call | flops 1 | bytes 1 | tf_op jit(solution)/shard_map/finish_pairs/pallas_call | solution.py:313
  44.6 0.0 collective-permute-done.7.refs_6_
  44.6 0.0 collective-permute-done.6.refs_5_
  44.6 0.0 collective-permute-done.5.refs_4_
  44.7 0.0 collective-permute-done.4.refs_3_
  44.7 6.6 %add_pairs.3 = (f32[2,768,1152]{2,1,0:T(8,128)S(1)}, f32[768,128]{1,0:T(8,128)S(1)}, bf16[768,1152]{1,0:T(8,128)(2,1)S(1)}) custom-call(s32[1]{0:T(128)} %bitcast.odd.refs_0_, f32[1]{0:T(128)S(6)} %copy.21.log_scale.refs_1_, f32[1]{0:T(128)S(6)} %copy.22.logit_bias.refs_2_, ...), custom_call_target="tpu_custom_call", output_to_operand_aliasing={{0}: (8, {}), {1}: (9, {})} | custom-call | flops 1 | bytes 1 | tf_op jit(solution)/shard_map/add_pairs/pallas_call | solution.py:286
  51.2 0.0 collective-permute-done.2.refs_3_
  51.2 5.2 %finish_pairs.3 = (f32[768]{0:T(1024)}, f32[768,1152]{1,0:T(8,128)}, f32[768,1152]{1,0:T(8,128)}) custom-call(s32[1]{0:T(128)} %bitcast.odd.refs_0_, f32[1]{0:T(128)S(6)} %copy.21.log_scale.refs_1_, f32[1]{0:T(128)S(6)} %copy.22.logit_bias.refs_2_, ...), custom_call_target="tpu_custom_call", output_to_operand_aliasing={{1}: (8, {}), {2}: (9, {})} | custom-call | flops 1 | bytes 1 | tf_op jit(solution)/shard_map/finish_pairs/pallas_call | solution.py:313
Async XLA Ops:
  2.1 31.0 %collective-permute-start.3 = (bf16[768,1152]{1,0:T(8,128)(2,1)S(1)}, bf16[768,1152]{1,0:T(8,128)(2,1)S(1)}, u32[]{:S(2)}, u32[]{:S(2)}) collective-permute-start(bf16[768,1152]{1,0:T(8,128)(2,1)S(1)} %pick.1.far), channel_id=1, source_target_pairs={{0,254},{1,3},{2,0},{3,5},{4,2},{5,7},{6,4},{7,9},{8,6},{9,11},{10... | collective-permute-start | bytes 5308424 | tf_op jit(solution)/shard_map/ppermute | solution.py:355
  6.3 13.4 %collective-permute-start = (bf16[400,1152]{1,0:T(8,128)(2,1)S(1)}, bf16[400,1152]{1,0:T(8,128)(2,1)S(1)}, u32[]{:S(2)}, u32[]{:S(2)}) collective-permute-start(bf16[400,1152]{1,0:T(8,128)(2,1)S(1)} %get-tuple-element.24), channel_id=1, source_target_pairs={{0,1},{1,0},{2,3},{3,2},{4,5},{5,4},{6,7},{7,6},{8,9},{9,8},{10,11... | collective-permute-start | bytes 2764808 | tf_op jit(solution)/shard_map/ppermute | solution.py:355
  16.3 3.3 %collective-permute-start.1 = (bf16[368,1152]{1,0:T(8,128)(2,1)S(1)}, bf16[368,1152]{1,0:T(8,128)(2,1)S(1)}, u32[]{:S(2)}, u32[]{:S(2)}) collective-permute-start(bf16[368,1152]{1,0:T(8,128)(2,1)S(1)} %get-tuple-element.25), channel_id=1, source_target_pairs={{0,1},{1,0},{2,3},{3,2},{4,5},{5,4},{6,7},{7,6},{8,9},{9,8},{10,11... | collective-permute-start | bytes 2543624 | tf_op jit(solution)/shard_map/ppermute | solution.py:355
  19.6 25.0 %collective-permute-start.7 = (bf16[400,1152]{1,0:T(8,128)(2,1)S(1)}, bf16[400,1152]{1,0:T(8,128)(2,1)S(1)}, u32[]{:S(2)}, u32[]{:S(2)}) collective-permute-start(bf16[400,1152]{1,0:T(8,128)(2,1)S(1)} %collective-permute-done.refs_3_), channel_id=1, source_target_pairs={{0,255},{1,2},{2,1},{3,4},{4,3},{5,6},{6,5},{7,8},{8,7},{9,10},{10... | collective-permute-start | bytes 2764808 | tf_op jit(solution)/shard_map/ppermute | solution.py:355
  25.2 26.0 %collective-permute-start.2 = (bf16[368,1152]{1,0:T(8,128)(2,1)S(1)}, bf16[368,1152]{1,0:T(8,128)(2,1)S(1)}, u32[]{:S(2)}, u32[]{:S(2)}) collective-permute-start(bf16[368,1152]{1,0:T(8,128)(2,1)S(1)} %collective-permute-done.1.refs_4_), channel_id=1, source_target_pairs={{0,255},{1,2},{2,1},{3,4},{4,3},{5,6},{6,5},{7,8},{8,7},{9,10},{10... | collective-permute-start | bytes 2543624 | tf_op jit(solution)/shard_map/ppermute | solution.py:355
  33.3 11.3 %collective-permute-start.6 = (bf16[256,1152]{1,0:T(8,128)(2,1)S(1)}, bf16[256,1152]{1,0:T(8,128)(2,1)S(1)}, u32[]{:S(2)}, u32[]{:S(2)}) collective-permute-start(bf16[256,1152]{1,0:T(8,128)(2,1)S(1)} %get-tuple-element.45), channel_id=1, source_target_pairs={{0,1},{1,0},{2,3},{3,2},{4,5},{5,4},{6,7},{7,6},{8,9},{9,8},{10,11... | collective-permute-start | bytes 1769480 | tf_op jit(solution)/shard_map/ppermute | solution.py:355
  37.5 7.2 %collective-permute-start.5 = (bf16[256,1152]{1,0:T(8,128)(2,1)S(1)}, bf16[256,1152]{1,0:T(8,128)(2,1)S(1)}, u32[]{:S(2)}, u32[]{:S(2)}) collective-permute-start(bf16[256,1152]{1,0:T(8,128)(2,1)S(1)} %get-tuple-element.46), channel_id=1, source_target_pairs={{0,1},{1,0},{2,3},{3,2},{4,5},{5,4},{6,7},{7,6},{8,9},{9,8},{10,11... | collective-permute-start | bytes 1769480 | tf_op jit(solution)/shard_map/ppermute | solution.py:355
  37.6 7.1 %collective-permute-start.4 = (bf16[256,1152]{1,0:T(8,128)(2,1)S(1)}, bf16[256,1152]{1,0:T(8,128)(2,1)S(1)}, u32[]{:S(2)}, u32[]{:S(2)}) collective-permute-start(bf16[256,1152]{1,0:T(8,128)(2,1)S(1)} %get-tuple-element.47), channel_id=1, source_target_pairs={{0,1},{1,0},{2,3},{3,2},{4,5},{5,4},{6,7},{7,6},{8,9},{9,8},{10,11... | collective-permute-start | bytes 1769480 | tf_op jit(solution)/shard_map/ppermute | solution.py:355

commit v5 on v4

--- a/solution.py
+++ b/solution.py
@@ -210,66 +210,69 @@
         loss[rows] = loss_in[rows] + jnp.where(has_loss, losses, 0.0)
 
 
-def add_kernel(*refs, side, pieces, fetch):
+def row_steps(count):
+    step = RB if count >= RB else TILE
+    return [slice(row, row + step) for row in range(0, RB, step)]
+
+
+def accumulate(side, rows, log_scale, grads, slopes, other_emb):
+    return grads[side, rows] + scale_row(log_scale, D) * matmul(slopes[rows], other_emb[...])
+
+
+def back_norm(total, raw):
+    unit, inverse = normalize(raw)
+    return (total - unit * jnp.sum(unit * total, axis=1, keepdims=True)) * inverse
+
+
+def add_kernel(*refs, side, pieces, passes):
     odd, log_scale, logit_bias, *others = refs[: 3 + pieces]
-    emb, grads_in, loss_in, *refs = refs[3 + pieces :]
+    emb, grads_in, loss_in, images, texts, *refs = refs[3 + pieces :]
     has_loss = odd[0] == (1 if side == NEAR else 0)
-    if fetch:
-        images, texts, grads, loss, raw, other_emb, slopes, raw_sem = refs
-        copy_if(has_loss, images, raw, raw_sem)
-        copy_if(jnp.logical_not(has_loss), texts, raw, raw_sem)
+    if passes:
+        finished, grads, loss, raw, image_grad, text_grad, *refs = refs
+        copy_if(jnp.logical_not(has_loss), finished, image_grad, refs[3])
+        copy_if(has_loss, finished, text_grad, refs[3])
     else:
-        grads, loss, other_emb, slopes = refs
+        grads, loss, raw, *refs = refs
+    other_emb, slopes, raw_sem = refs[:3]
+    copy_if(has_loss, images, raw, raw_sem)
+    copy_if(jnp.logical_not(has_loss), texts, raw, raw_sem)
     valid = embed_all(others, other_emb)
     score(side, has_loss, log_scale, logit_bias, emb, loss_in, loss, other_emb, slopes, valid)
-    scale_wide = scale_row(log_scale, D)
-    step = RB if other_emb.shape[0] >= RB else TILE
-    for row in range(0, RB, step):
-        rows = slice(row, row + step)
-        grads[side, rows] = grads_in[side, rows] + scale_wide * matmul(
-            slopes[rows], other_emb[...]
-        )
-    if fetch:
-        pltpu.make_async_copy(images, raw, raw_sem).wait()
-
-
-def finish_kernel(*refs, side):
-    odd, log_scale, logit_bias, other, emb, grads, loss_in, raw = refs[:8]
-    if side == FAR:
-        refs = refs[2:]
-    loss, image_grad, text_grad, *scratch = refs[8:]
-    other_emb, slopes, finished, out_sems = scratch[:4]
-    of_images = odd[0] == (1 if side == NEAR else 0)
+    for rows in row_steps(other_emb.shape[0]):
+        grads[side, rows] = accumulate(side, rows, log_scale, grads_in, slopes, other_emb)
+    pltpu.make_async_copy(images, raw, raw_sem).wait()
+    if passes:
+        pltpu.make_async_copy(finished, image_grad, refs[3]).wait()
+
+
+def near_kernel(*refs):
+    odd, log_scale, logit_bias, other, emb, grads, loss_in, raw, *refs = refs
+    loss, finished, other_emb, slopes = refs
     valid = embed_all([other], other_emb)
-    sums = loss if side == NEAR else scratch[4]
-    score(side, of_images, log_scale, logit_bias, emb, loss_in, sums, other_emb, slopes, valid)
-    scale_wide = scale_row(log_scale, D)
-
-    def accumulate(rows):
-        finished[rows] = grads[side, rows] + scale_wide * matmul(slopes[rows], other_emb[...])
-
-    def finish(here):
-        total = finished[here]
-        unit, inverse = normalize(raw[here])
-        finished[here] = (total - unit * jnp.sum(unit * total, axis=1, keepdims=True)) * inverse
-
-    if side == NEAR:
-        accumulate(slice(0, RB))
+    score(NEAR, odd[0] == 1, log_scale, logit_bias, emb, loss_in, loss, other_emb, slopes, valid)
+    finished[...] = accumulate(NEAR, slice(0, RB), log_scale, grads, slopes, other_emb)
+    for row in range(PARTS):
+        finished[tile(row)] = back_norm(finished[tile(row)], raw[tile(row)])
+
+
+def far_kernel(*refs):
+    odd, log_scale, logit_bias, other, emb, grads, loss_in, raw, _, _, *refs = refs
+    row_loss, image_grad, text_grad, other_emb, slopes, finished, sums, sems = refs
+    far_images = odd[0] == 0
+    valid = embed_all([other], other_emb)
+    score(FAR, far_images, log_scale, logit_bias, emb, loss_in, sums, other_emb, slopes, valid)
     for row in range(PARTS):
         here = tile(row)
-        if side == FAR:
-            accumulate(here)
-        finish(here)
-        copy_if(of_images, finished.at[here], image_grad.at[here], out_sems.at[row])
-        copy_if(
-            jnp.logical_not(of_images), finished.at[here], text_grad.at[here], out_sems.at[row]
-        )
-    if side == FAR:
-        for row in range(PARTS):
-            loss[tile(row)] = jnp.sum(sums[tile(row)].T, axis=0) * (1.0 / (STEPS * RB))
+        total = accumulate(FAR, here, log_scale, grads, slopes, other_emb)
+        finished[here] = back_norm(total, raw[here])
+        copy_if(far_images, finished.at[here], image_grad.at[here], sems.at[row])
+        copy_if(jnp.logical_not(far_images), finished.at[here], text_grad.at[here], sems.at[row])
+    for row in range(PARTS):
+        row_loss[tile(row)] = jnp.sum(sums[tile(row)].T, axis=0) * (1.0 / (STEPS * RB))
     for row in range(PARTS):
         here = tile(row)
-        pltpu.make_async_copy(finished.at[here], image_grad.at[here], out_sems.at[row]).wait()
+        pltpu.make_async_copy(finished.at[here], image_grad.at[here], sems.at[row]).wait()
 
 
 def score_scratch(count):
@@ -279,20 +282,28 @@
     ]
 
 
-def add_pairs(side, scalars, others, emb, grads, loss, fetch=()):
+def block_grad():
+    return jax.ShapeDtypeStruct((RB, D), jnp.float32)
+
+
+def add_pairs(side, scalars, others, emb, grads, loss, images, texts, finished=None):
     count = sum(other.shape[0] for other in others)
+    passes = finished is not None
     at = 4 + len(others)
-    raw = pltpu.VMEM((RB, D), jnp.bfloat16)
-    return pl.pallas_call(
-        functools.partial(add_kernel, side=side, pieces=len(others), fetch=bool(fetch)),
-        in_specs=[SCALARS] * 3 + [RESIDENT] * (3 + len(others)) + [ANYWHERE] * len(fetch),
-        out_specs=[RESIDENT] * (3 if fetch else 2),
+    return pl.pallas_call(
+        functools.partial(add_kernel, side=side, pieces=len(others), passes=passes),
+        in_specs=[SCALARS] * 3
+        + [RESIDENT] * (3 + len(others))
+        + [ANYWHERE] * 2
+        + [RESIDENT] * passes,
+        out_specs=[RESIDENT] * 3 + [ANYWHERE] * (2 * passes),
         out_shape=[
             pltpu.VMEM(grads.shape, jnp.float32),
             pltpu.VMEM(loss.shape, jnp.float32),
+            pltpu.VMEM((RB, D), jnp.bfloat16),
         ]
-        + ([raw] if fetch else []),
-        scratch_shapes=score_scratch(count) + ([pltpu.SemaphoreType.DMA] if fetch else []),
+        + [block_grad()] * (2 * passes),
+        scratch_shapes=score_scratch(count) + [pltpu.SemaphoreType.DMA] * (1 + passes),
         input_output_aliases={at: 0, at + 1: 1},
         compiler_params=pltpu.CompilerParams(vmem_limit_bytes=VMEM_LIMIT),
         cost_estimate=NO_COST,
@@ -303,43 +314,46 @@
         kept(emb),
         kept(grads),
         kept(loss),
-        *map(in_hbm, fetch),
+        in_hbm(images),
+        in_hbm(texts),
+        *([kept(finished)] if passes else []),
     )
 
 
-def finish_pairs(side, scalars, other, emb, grads, loss, raw, outs=()):
-    count = other.shape[0]
-    last = side == FAR
-    return pl.pallas_call(
-        functools.partial(finish_kernel, side=side),
-        in_specs=[SCALARS] * 3 + [RESIDENT] * 5 + [ANYWHERE] * len(outs),
+def near_pairs(scalars, other, emb, grads, loss, raw):
+    return pl.pallas_call(
+        near_kernel,
+        in_specs=[SCALARS] * 3 + [RESIDENT] * 5,
+        out_specs=[RESIDENT] * 2,
+        out_shape=[
+            pltpu.VMEM(loss.shape, jnp.float32),
+            pltpu.VMEM((RB, D), jnp.float32),
+        ],
+        scratch_shapes=score_scratch(other.shape[0]),
+        input_output_aliases={6: 0},
+        compiler_params=pltpu.CompilerParams(vmem_limit_bytes=VMEM_LIMIT),
+        cost_estimate=NO_COST,
+        name="near_pairs",
+    )(*scalars, kept(other), kept(emb), kept(grads), kept(loss), kept(raw))
+
+
+def far_pairs(scalars, other, emb, grads, loss, raw, outs):
+    return pl.pallas_call(
+        far_kernel,
+        in_specs=[SCALARS] * 3 + [RESIDENT] * 5 + [ANYWHERE] * 2,
         out_specs=[RESIDENT, ANYWHERE, ANYWHERE],
-        out_shape=[
-            jax.ShapeDtypeStruct((RB,), jnp.float32)
-            if last
-            else pltpu.VMEM(loss.shape, jnp.float32),
-            jax.ShapeDtypeStruct((RB, D), jnp.float32),
-            jax.ShapeDtypeStruct((RB, D), jnp.float32),
-        ],
-        scratch_shapes=score_scratch(count)
+        out_shape=[jax.ShapeDtypeStruct((RB,), jnp.float32), block_grad(), block_grad()],
+        scratch_shapes=score_scratch(other.shape[0])
         + [
             pltpu.VMEM((RB, D), jnp.float32),
+            pltpu.VMEM(loss.shape, jnp.float32),
             pltpu.SemaphoreType.DMA((PARTS,)),
-        ]
-        + ([pltpu.VMEM(loss.shape, jnp.float32)] if last else []),
-        input_output_aliases={8: 1, 9: 2} if last else {6: 0},
+        ],
+        input_output_aliases={8: 1, 9: 2},
         compiler_params=pltpu.CompilerParams(vmem_limit_bytes=VMEM_LIMIT),
         cost_estimate=NO_COST,
-        name="finish_pairs",
-    )(
-        *scalars,
-        kept(other),
-        kept(emb),
-        kept(grads),
-        kept(loss),
-        kept(raw),
-        *outs,
-    )
+        name="far_pairs",
+    )(*scalars, kept(other), kept(emb), kept(grads), kept(loss), kept(raw), *outs)
 
 
 def per_device(images, texts, log_scale, logit_bias):
@@ -365,16 +379,16 @@
     beside_tail, grads = lax.optimization_barrier((beside_tail, grads))
     near_tail_other = send(beside_tail, second)
     grads, loss, raw = add_pairs(
-        NEAR, scalars, [beside_head, beside_tail], emb, grads, loss, (images, texts)
+        NEAR, scalars, [beside_head, beside_tail], emb, grads, loss, images, texts
     )
     far_other, grads = lax.optimization_barrier((far_other, grads))
     far_beside = [send(far_other[at : at + PIECE], across) for at in range(0, RB, PIECE)]
-    loss, *outs = finish_pairs(NEAR, scalars, far_other, emb, grads, loss, raw)
-    grads, loss, raw = add_pairs(
-        FAR, scalars, [*far_beside, near_head_other], emb, grads, loss, (images, texts)
+    loss, finished = near_pairs(scalars, far_other, emb, grads, loss, raw)
+    grads, loss, raw, *outs = add_pairs(
+        FAR, scalars, [*far_beside, near_head_other], emb, grads, loss, images, texts, finished
     )
-    row_loss, image_grad, text_grad = finish_pairs(
-        FAR, scalars, near_tail_other, emb, grads, loss, raw, outs
+    row_loss, image_grad, text_grad = far_pairs(
+        scalars, near_tail_other, emb, grads, loss, raw, outs
     )
     return (row_loss, image_grad, text_grad)
 

time: 56.7 us -> 55.6 us (0.981)
  Pallas kernels: 31.6 us -> 30.3 us
    pallas_call x2, Pallas kernels: 11.8 us -> 10.5 us  [the longest x1 5.3 us: far_pairs(): pl.pallas_call(far_kernel, in_specs=[SCALARS] * 3 + [RESIDENT] * 5 + [ANY...]
  transfers between devices with their start and end apart: 8 -> 8, of which waited for: 2 -> 2; matrix products, arithmetic and copies ran while one was open for 0% -> 0% of each run, Pallas kernels for 44% -> 43%
where the time goes in v5:
time: 55.6 us; the launch traced here: 55.3 us
  Pallas kernels  30.3 us (54%)
  starting transfers between devices  19 us (34%)
  waiting for transfers between devices  3.68 us (7%)
  between operations  2.19 us (4%)
    ppermute x8, starting transfers between devices, send(): return lax.ppermute(block, 'blk', pairs)  19 us
    pallas_call x2, Pallas kernels, add_pairs(): pl.pallas_call(functools.partial(add_kernel, side=side, pieces=len(others...  10.8 us
    pallas_call x1, Pallas kernels, own_pairs(): pl.pallas_call(own_kernel, in_specs=[SCALARS] * 3 + [RESIDENT], out_specs...  5.59 us
    pallas_call x1, Pallas kernels, far_pairs(): pl.pallas_call(far_kernel, in_specs=[SCALARS] * 3 + [RESIDENT] * 5 + [ANY...  5.3 us
    pallas_call x1, Pallas kernels, near_pairs(): pl.pallas_call(near_kernel, in_specs=[SCALARS] * 3 + [RESIDENT] * 5, out_...  5.17 us
    ppermute x8, waiting for transfers between devices, send(): return lax.ppermute(block, 'blk', pairs)  3.68 us
    pallas_call x1, Pallas kernels, prepare(): pl.pallas_call(prepare_kernel, in_specs=[SCALARS, ANYWHERE, ANYWHERE, RES...  2 us
    pallas_call x1, Pallas kernels, pick(): pl.pallas_call(pick_kernel, in_specs=[SCALARS, ANYWHERE, ANYWHERE], out_s...  1.49 us
  transfers between devices with their start and end apart: 8, of which 2 were waited for; matrix products, arithmetic and copies ran while one was open for 0% of the time, Pallas kernels for 43%

profile of v5, /device:TPU:1, one launch (start us, length us, event | category | flops | bytes accessed | tf_op | source)
XLA Modules:
  0.0 55.3 jit_solution(16754136506017209259)
XLA Ops:
  0.6 1.5 %pick.1.far = bf16[768,1152]{1,0:T(8,128)(2,1)S(1)} custom-call(s32[1]{0:T(128)} %bitcast.odd.refs_0_, bf16[768,1152]{1,0:T(8,128)(2,1)} %refs_10_.1, bf16[768,1152]{1,0:T(8,128)(2,1)} %refs_11_.1), custom_call_target="tpu_custom_call" | custom-call | flops 1 | bytes 1 | tf_op jit(solution)/shard_map/pick/pallas_call | solution.py:83
  2.1 2.1 %collective-permute-start.3 = (bf16[768,1152]{1,0:T(8,128)(2,1)S(1)}, bf16[768,1152]{1,0:T(8,128)(2,1)S(1)}, u32[]{:S(2)}, u32[]{:S(2)}) collective-permute-start(bf16[768,1152]{1,0:T(8,128)(2,1)S(1)} %pick.1.far), channel_id=1, source_target_pairs={{0,254},{1,3},{2,0},{3,5},{4,2},{5,7},{6,4},{7,9},{8,6},{9,11},{10... | collective-permute-start | bytes 5308424 | tf_op jit(solution)/shard_map/ppermute | solution.py:369
  4.3 2.0 %prepare.1 = (bf16[2,768,1152]{2,1,0:T(8,128)(2,1)S(1)}, bf16[400,1152]{1,0:T(8,128)(2,1)S(1)}, bf16[368,1152]{1,0:T(8,128)(2,1)S(1)}) custom-call(s32[1]{0:T(128)} %bitcast.odd.refs_0_, bf16[768,1152]{1,0:T(8,128)(2,1)} %refs_10_.1, bf16[768,1152]{1,0:T(8,128)(2,1)} %refs_11_.1, bf16[768,1152]{1,0:T(8,128)(2,1)S(1)} %pick.1.far), custom_call_target="tpu_custom_call" | custom-call | flops 1 | bytes 1 | tf_op jit(solution)/shard_map/prepare/pallas_call | solution.py:113
  6.3 10.1 %collective-permute-start = (bf16[400,1152]{1,0:T(8,128)(2,1)S(1)}, bf16[400,1152]{1,0:T(8,128)(2,1)S(1)}, u32[]{:S(2)}, u32[]{:S(2)}) collective-permute-start(bf16[400,1152]{1,0:T(8,128)(2,1)S(1)} %get-tuple-element.25), channel_id=1, source_target_pairs={{0,1},{1,0},{2,3},{3,2},{4,5},{5,4},{6,7},{7,6},{8,9},{9,8},{10,11... | collective-permute-start | bytes 2764808 | tf_op jit(solution)/shard_map/ppermute | solution.py:369
  16.3 0.1 collective-permute-start.1
  17.7 1.9 %collective-permute-done.1.refs_4_ = bf16[368,1152]{1,0:T(8,128)(2,1)S(1)} collective-permute-done((bf16[368,1152]{1,0:T(8,128)(2,1)S(1)}, bf16[368,1152]{1,0:T(8,128)(2,1)S(1)}, u32[]{:S(2)}, u32[]{:S(2)}) %collective-permute-start.1) | collective-permute-done | bytes 847904 | tf_op jit(solution)/shard_map/ppermute | solution.py:369
  19.6 0.0 collective-permute-done.refs_3_
  19.6 0.0 collective-permute-start.7
  19.6 5.6 %own_pairs.1 = (f32[2,768,1152]{2,1,0:T(8,128)S(1)}, f32[768,128]{1,0:T(8,128)S(1)}) custom-call(s32[1]{0:T(128)} %bitcast.odd.refs_0_, f32[1]{0:T(128)S(6)} %copy.21.log_scale.refs_1_, f32[1]{0:T(128)S(6)} %copy.22.logit_bias.refs_2_, bf16[2,768,1152]{2,1,0:T(8,128)(2,1)S(1)} %get-tuple-element.29.emb.refs_5_.refs_4_.refs_7_), custom_call_target="tpu_custom_call" | custom-call | flops 1 | bytes 1 | tf_op jit(solution)/shard_map/own_pairs/pallas_call | solution.py:158
  25.2 2.0 %collective-permute-start.2 = (bf16[368,1152]{1,0:T(8,128)(2,1)S(1)}, bf16[368,1152]{1,0:T(8,128)(2,1)S(1)}, u32[]{:S(2)}, u32[]{:S(2)}) collective-permute-start(bf16[368,1152]{1,0:T(8,128)(2,1)S(1)} %collective-permute-done.1.refs_4_), channel_id=1, source_target_pairs={{0,255},{1,2},{2,1},{3,4},{4,3},{5,6},{6,5},{7,8},{8,7},{9,10},{10... | collective-permute-start | bytes 2543624 | tf_op jit(solution)/shard_map/ppermute | solution.py:369
  27.2 4.2 %add_pairs.2 = (f32[2,768,1152]{2,1,0:T(8,128)S(1)}, f32[768,128]{1,0:T(8,128)S(1)}, bf16[768,1152]{1,0:T(8,128)(2,1)S(1)}) custom-call(s32[1]{0:T(128)} %bitcast.odd.refs_0_, f32[1]{0:T(128)S(6)} %copy.21.log_scale.refs_1_, f32[1]{0:T(128)S(6)} %copy.22.logit_bias.refs_2_, ...), custom_call_target="tpu_custom_call", output_to_operand_aliasing={{0}: (6, {}), {1}: (7, {})} | custom-call | flops 1 | bytes 1 | tf_op jit(solution)/shard_map/add_pairs/pallas_call | solution.py:293
  31.4 1.7 %collective-permute-done.3.refs_3_ = bf16[768,1152]{1,0:T(8,128)(2,1)S(1)} collective-permute-done((bf16[768,1152]{1,0:T(8,128)(2,1)S(1)}, bf16[768,1152]{1,0:T(8,128)(2,1)S(1)}, u32[]{:S(2)}, u32[]{:S(2)}) %collective-permute-start.3) | collective-permute-done | bytes 1769504 | tf_op jit(solution)/shard_map/ppermute | solution.py:369
  33.2 0.1 fusion
  33.3 4.2 %collective-permute-start.6 = (bf16[256,1152]{1,0:T(8,128)(2,1)S(1)}, bf16[256,1152]{1,0:T(8,128)(2,1)S(1)}, u32[]{:S(2)}, u32[]{:S(2)}) collective-permute-start(bf16[256,1152]{1,0:T(8,128)(2,1)S(1)} %get-tuple-element.47), channel_id=1, source_target_pairs={{0,1},{1,0},{2,3},{3,2},{4,5},{5,4},{6,7},{7,6},{8,9},{9,8},{10,11... | collective-permute-start | bytes 1769480 | tf_op jit(solution)/shard_map/ppermute | solution.py:369
  37.5 0.1 collective-permute-start.5
  37.6 0.4 collective-permute-start.4
  38.0 5.2 %near_pairs.1 = (f32[768,128]{1,0:T(8,128)S(1)}, f32[768,1152]{1,0:T(8,128)S(1)}) custom-call(s32[1]{0:T(128)} %bitcast.odd.refs_0_, f32[1]{0:T(128)S(6)} %copy.21.log_scale.refs_1_, f32[1]{0:T(128)S(6)} %copy.22.logit_bias.refs_2_, bf16[768,1152]{1,0:T(8,128)(2,1)S(1)} %collective-permute-done.3.refs_3_, ...), custom_call_target="tpu_custom_call", output_to_operand_aliasing={{0}: (6, {})} | custom-call | flops 1 | bytes 1 | tf_op jit(solution)/shard_map/near_pairs/pallas_call | solution.py:324
  43.2 0.0 collective-permute-done.7.refs_6_
  43.2 0.0 collective-permute-done.6.refs_5_
  43.2 0.0 collective-permute-done.5.refs_4_
  43.2 0.0 collective-permute-done.4.refs_3_
  43.2 6.6 %add_pairs.3 = (f32[2,768,1152]{2,1,0:T(8,128)S(1)}, f32[768,128]{1,0:T(8,128)S(1)}, bf16[768,1152]{1,0:T(8,128)(2,1)S(1)}, f32[768,1152]{1,0:T(8,128)}, f32[768,1152]{1,0:T(8,128)}) custom-call(s32[1]{0:T(128)} %bitcast.odd.refs_0_, f32[1]{0:T(128)S(6)} %copy.21.log_scale.refs_1_, ...), custom_call_target="tpu_custom_call", output_to_operand_aliasing={{0}: (8, {}), {1}: (9, {})} | custom-call | flops 1 | bytes 1 | tf_op jit(solution)/shard_map/add_pairs/pallas_call | solution.py:293
  49.8 0.0 collective-permute-done.2.refs_3_
  49.8 5.3 %far_pairs.1 = (f32[768]{0:T(1024)}, f32[768,1152]{1,0:T(8,128)}, f32[768,1152]{1,0:T(8,128)}) custom-call(s32[1]{0:T(128)} %bitcast.odd.refs_0_, f32[1]{0:T(128)S(6)} %copy.21.log_scale.refs_1_, f32[1]{0:T(128)S(6)} %copy.22.logit_bias.refs_2_, bf16[368,1152]{1,0:T(8,128)(2,1)S(1)} %collective-permute-done.2.refs_3_, ...), custom_call_target="tpu_custom_call", output_to_operand_aliasing={{1}: (8, {}), {2}: (9, {})} | custom-call | flops 1 | bytes 1 | tf_op jit(solution)/shard_map/far_pairs/pallas_call | solution.py:341
Async XLA Ops:
  2.1 31.0 %collective-permute-start.3 = (bf16[768,1152]{1,0:T(8,128)(2,1)S(1)}, bf16[768,1152]{1,0:T(8,128)(2,1)S(1)}, u32[]{:S(2)}, u32[]{:S(2)}) collective-permute-start(bf16[768,1152]{1,0:T(8,128)(2,1)S(1)} %pick.1.far), channel_id=1, source_target_pairs={{0,254},{1,3},{2,0},{3,5},{4,2},{5,7},{6,4},{7,9},{8,6},{9,11},{10... | collective-permute-start | bytes 5308424 | tf_op jit(solution)/shard_map/ppermute | solution.py:369
  6.3 13.4 %collective-permute-start = (bf16[400,1152]{1,0:T(8,128)(2,1)S(1)}, bf16[400,1152]{1,0:T(8,128)(2,1)S(1)}, u32[]{:S(2)}, u32[]{:S(2)}) collective-permute-start(bf16[400,1152]{1,0:T(8,128)(2,1)S(1)} %get-tuple-element.25), channel_id=1, source_target_pairs={{0,1},{1,0},{2,3},{3,2},{4,5},{5,4},{6,7},{7,6},{8,9},{9,8},{10,11... | collective-permute-start | bytes 2764808 | tf_op jit(solution)/shard_map/ppermute | solution.py:369
  16.3 3.3 %collective-permute-start.1 = (bf16[368,1152]{1,0:T(8,128)(2,1)S(1)}, bf16[368,1152]{1,0:T(8,128)(2,1)S(1)}, u32[]{:S(2)}, u32[]{:S(2)}) collective-permute-start(bf16[368,1152]{1,0:T(8,128)(2,1)S(1)} %get-tuple-element.26), channel_id=1, source_target_pairs={{0,1},{1,0},{2,3},{3,2},{4,5},{5,4},{6,7},{7,6},{8,9},{9,8},{10,11... | collective-permute-start | bytes 2543624 | tf_op jit(solution)/shard_map/ppermute | solution.py:369
  19.6 23.5 %collective-permute-start.7 = (bf16[400,1152]{1,0:T(8,128)(2,1)S(1)}, bf16[400,1152]{1,0:T(8,128)(2,1)S(1)}, u32[]{:S(2)}, u32[]{:S(2)}) collective-permute-start(bf16[400,1152]{1,0:T(8,128)(2,1)S(1)} %collective-permute-done.refs_3_), channel_id=1, source_target_pairs={{0,255},{1,2},{2,1},{3,4},{4,3},{5,6},{6,5},{7,8},{8,7},{9,10},{10... | collective-permute-start | bytes 2764808 | tf_op jit(solution)/shard_map/ppermute | solution.py:369
  25.2 24.6 %collective-permute-start.2 = (bf16[368,1152]{1,0:T(8,128)(2,1)S(1)}, bf16[368,1152]{1,0:T(8,128)(2,1)S(1)}, u32[]{:S(2)}, u32[]{:S(2)}) collective-permute-start(bf16[368,1152]{1,0:T(8,128)(2,1)S(1)} %collective-permute-done.1.refs_4_), channel_id=1, source_target_pairs={{0,255},{1,2},{2,1},{3,4},{4,3},{5,6},{6,5},{7,8},{8,7},{9,10},{10... | collective-permute-start | bytes 2543624 | tf_op jit(solution)/shard_map/ppermute | solution.py:369
  33.3 9.9 %collective-permute-start.6 = (bf16[256,1152]{1,0:T(8,128)(2,1)S(1)}, bf16[256,1152]{1,0:T(8,128)(2,1)S(1)}, u32[]{:S(2)}, u32[]{:S(2)}) collective-permute-start(bf16[256,1152]{1,0:T(8,128)(2,1)S(1)} %get-tuple-element.47), channel_id=1, source_target_pairs={{0,1},{1,0},{2,3},{3,2},{4,5},{5,4},{6,7},{7,6},{8,9},{9,8},{10,11... | collective-permute-start | bytes 1769480 | tf_op jit(solution)/shard_map/ppermute | solution.py:369
  37.5 5.7 %collective-permute-start.5 = (bf16[256,1152]{1,0:T(8,128)(2,1)S(1)}, bf16[256,1152]{1,0:T(8,128)(2,1)S(1)}, u32[]{:S(2)}, u32[]{:S(2)}) collective-permute-start(bf16[256,1152]{1,0:T(8,128)(2,1)S(1)} %get-tuple-element.48), channel_id=1, source_target_pairs={{0,1},{1,0},{2,3},{3,2},{4,5},{5,4},{6,7},{7,6},{8,9},{9,8},{10,11... | collective-permute-start | bytes 1769480 | tf_op jit(solution)/shard_map/ppermute | solution.py:369
  37.6 5.6 %collective-permute-start.4 = (bf16[256,1152]{1,0:T(8,128)(2,1)S(1)}, bf16[256,1152]{1,0:T(8,128)(2,1)S(1)}, u32[]{:S(2)}, u32[]{:S(2)}) collective-permute-start(bf16[256,1152]{1,0:T(8,128)(2,1)S(1)} %get-tuple-element.49), channel_id=1, source_target_pairs={{0,1},{1,0},{2,3},{3,2},{4,5},{5,4},{6,7},{7,6},{8,9},{9,8},{10,11... | collective-permute-start | bytes 1769480 | tf_op jit(solution)/shard_map/ppermute | solution.py:369

commit v6 on v5

--- a/solution.py
+++ b/solution.py
@@ -220,8 +220,10 @@
 
 
 def back_norm(total, raw):
-    unit, inverse = normalize(raw)
-    return (total - unit * jnp.sum(unit * total, axis=1, keepdims=True)) * inverse
+    widened = raw.astype(jnp.float32)
+    inverse = lax.rsqrt(jnp.sum(widened * widened, axis=1, keepdims=True) + EPS)
+    along = jnp.sum(widened * total, axis=1, keepdims=True)
+    return total * inverse - widened * (inverse * (inverse * (inverse * along)))
 
 
 def add_kernel(*refs, side, pieces, passes):

time: 55.6 us -> 55.5 us (level)
  no operation moved by 1% of the time
where the time goes in v6:
time: 55.5 us; the launch traced here: 55 us
  Pallas kernels  30.1 us (54%)
  starting transfers between devices  19 us (34%)
  waiting for transfers between devices  3.68 us (7%)
  between operations  2.19 us (4%)
    ppermute x8, starting transfers between devices, send(): return lax.ppermute(block, 'blk', pairs)  19 us
    pallas_call x2, Pallas kernels, add_pairs(): pl.pallas_call(functools.partial(add_kernel, side=side, pieces=len(others...  10.8 us
    pallas_call x1, Pallas kernels, own_pairs(): pl.pallas_call(own_kernel, in_specs=[SCALARS] * 3 + [RESIDENT], out_specs...  5.59 us
    pallas_call x1, Pallas kernels, far_pairs(): pl.pallas_call(far_kernel, in_specs=[SCALARS] * 3 + [RESIDENT] * 5 + [ANY...  5.16 us
    pallas_call x1, Pallas kernels, near_pairs(): pl.pallas_call(near_kernel, in_specs=[SCALARS] * 3 + [RESIDENT] * 5, out_...  5.08 us
    ppermute x8, waiting for transfers between devices, send(): return lax.ppermute(block, 'blk', pairs)  3.68 us
    pallas_call x1, Pallas kernels, prepare(): pl.pallas_call(prepare_kernel, in_specs=[SCALARS, ANYWHERE, ANYWHERE, RES...  2 us
    pallas_call x1, Pallas kernels, pick(): pl.pallas_call(pick_kernel, in_specs=[SCALARS, ANYWHERE, ANYWHERE], out_s...  1.49 us
  transfers between devices with their start and end apart: 8, of which 2 were waited for; matrix products, arithmetic and copies ran while one was open for 0% of the time, Pallas kernels for 43%

profile of v6, /device:TPU:1, one launch (start us, length us, event | category | flops | bytes accessed | tf_op | source)
XLA Modules:
  0.0 55.0 jit_solution(7145701158681296720)
XLA Ops:
  0.6 1.5 %pick.1.far = bf16[768,1152]{1,0:T(8,128)(2,1)S(1)} custom-call(s32[1]{0:T(128)} %bitcast.odd.refs_0_, bf16[768,1152]{1,0:T(8,128)(2,1)} %refs_10_.1, bf16[768,1152]{1,0:T(8,128)(2,1)} %refs_11_.1), custom_call_target="tpu_custom_call" | custom-call | flops 1 | bytes 1 | tf_op jit(solution)/shard_map/pick/pallas_call | solution.py:83
  2.1 2.1 %collective-permute-start.3 = (bf16[768,1152]{1,0:T(8,128)(2,1)S(1)}, bf16[768,1152]{1,0:T(8,128)(2,1)S(1)}, u32[]{:S(2)}, u32[]{:S(2)}) collective-permute-start(bf16[768,1152]{1,0:T(8,128)(2,1)S(1)} %pick.1.far), channel_id=1, source_target_pairs={{0,254},{1,3},{2,0},{3,5},{4,2},{5,7},{6,4},{7,9},{8,6},{9,11},{10... | collective-permute-start | bytes 5308424 | tf_op jit(solution)/shard_map/ppermute | solution.py:371
  4.3 2.0 %prepare.1 = (bf16[2,768,1152]{2,1,0:T(8,128)(2,1)S(1)}, bf16[400,1152]{1,0:T(8,128)(2,1)S(1)}, bf16[368,1152]{1,0:T(8,128)(2,1)S(1)}) custom-call(s32[1]{0:T(128)} %bitcast.odd.refs_0_, bf16[768,1152]{1,0:T(8,128)(2,1)} %refs_10_.1, bf16[768,1152]{1,0:T(8,128)(2,1)} %refs_11_.1, bf16[768,1152]{1,0:T(8,128)(2,1)S(1)} %pick.1.far), custom_call_target="tpu_custom_call" | custom-call | flops 1 | bytes 1 | tf_op jit(solution)/shard_map/prepare/pallas_call | solution.py:113
  6.3 10.1 %collective-permute-start = (bf16[400,1152]{1,0:T(8,128)(2,1)S(1)}, bf16[400,1152]{1,0:T(8,128)(2,1)S(1)}, u32[]{:S(2)}, u32[]{:S(2)}) collective-permute-start(bf16[400,1152]{1,0:T(8,128)(2,1)S(1)} %get-tuple-element.25), channel_id=1, source_target_pairs={{0,1},{1,0},{2,3},{3,2},{4,5},{5,4},{6,7},{7,6},{8,9},{9,8},{10,11... | collective-permute-start | bytes 2764808 | tf_op jit(solution)/shard_map/ppermute | solution.py:371
  16.3 0.1 collective-permute-start.1
  17.7 1.9 %collective-permute-done.1.refs_4_ = bf16[368,1152]{1,0:T(8,128)(2,1)S(1)} collective-permute-done((bf16[368,1152]{1,0:T(8,128)(2,1)S(1)}, bf16[368,1152]{1,0:T(8,128)(2,1)S(1)}, u32[]{:S(2)}, u32[]{:S(2)}) %collective-permute-start.1) | collective-permute-done | bytes 847904 | tf_op jit(solution)/shard_map/ppermute | solution.py:371
  19.6 0.0 collective-permute-done.refs_3_
  19.6 0.0 collective-permute-start.7
  19.6 5.6 %own_pairs.1 = (f32[2,768,1152]{2,1,0:T(8,128)S(1)}, f32[768,128]{1,0:T(8,128)S(1)}) custom-call(s32[1]{0:T(128)} %bitcast.odd.refs_0_, f32[1]{0:T(128)S(6)} %copy.21.log_scale.refs_1_, f32[1]{0:T(128)S(6)} %copy.22.logit_bias.refs_2_, bf16[2,768,1152]{2,1,0:T(8,128)(2,1)S(1)} %get-tuple-element.29.emb.refs_5_.refs_4_.refs_7_), custom_call_target="tpu_custom_call" | custom-call | flops 1 | bytes 1 | tf_op jit(solution)/shard_map/own_pairs/pallas_call | solution.py:158
  25.2 2.0 %collective-permute-start.2 = (bf16[368,1152]{1,0:T(8,128)(2,1)S(1)}, bf16[368,1152]{1,0:T(8,128)(2,1)S(1)}, u32[]{:S(2)}, u32[]{:S(2)}) collective-permute-start(bf16[368,1152]{1,0:T(8,128)(2,1)S(1)} %collective-permute-done.1.refs_4_), channel_id=1, source_target_pairs={{0,255},{1,2},{2,1},{3,4},{4,3},{5,6},{6,5},{7,8},{8,7},{9,10},{10... | collective-permute-start | bytes 2543624 | tf_op jit(solution)/shard_map/ppermute | solution.py:371
  27.2 4.2 %add_pairs.2 = (f32[2,768,1152]{2,1,0:T(8,128)S(1)}, f32[768,128]{1,0:T(8,128)S(1)}, bf16[768,1152]{1,0:T(8,128)(2,1)S(1)}) custom-call(s32[1]{0:T(128)} %bitcast.odd.refs_0_, f32[1]{0:T(128)S(6)} %copy.21.log_scale.refs_1_, f32[1]{0:T(128)S(6)} %copy.22.logit_bias.refs_2_, ...), custom_call_target="tpu_custom_call", output_to_operand_aliasing={{0}: (6, {}), {1}: (7, {})} | custom-call | flops 1 | bytes 1 | tf_op jit(solution)/shard_map/add_pairs/pallas_call | solution.py:295
  31.4 1.7 %collective-permute-done.3.refs_3_ = bf16[768,1152]{1,0:T(8,128)(2,1)S(1)} collective-permute-done((bf16[768,1152]{1,0:T(8,128)(2,1)S(1)}, bf16[768,1152]{1,0:T(8,128)(2,1)S(1)}, u32[]{:S(2)}, u32[]{:S(2)}) %collective-permute-start.3) | collective-permute-done | bytes 1769504 | tf_op jit(solution)/shard_map/ppermute | solution.py:371
  33.2 0.1 fusion
  33.3 4.2 %collective-permute-start.6 = (bf16[256,1152]{1,0:T(8,128)(2,1)S(1)}, bf16[256,1152]{1,0:T(8,128)(2,1)S(1)}, u32[]{:S(2)}, u32[]{:S(2)}) collective-permute-start(bf16[256,1152]{1,0:T(8,128)(2,1)S(1)} %get-tuple-element.47), channel_id=1, source_target_pairs={{0,1},{1,0},{2,3},{3,2},{4,5},{5,4},{6,7},{7,6},{8,9},{9,8},{10,11... | collective-permute-start | bytes 1769480 | tf_op jit(solution)/shard_map/ppermute | solution.py:371
  37.5 0.1 collective-permute-start.5
  37.6 0.4 collective-permute-start.4
  38.0 5.1 %near_pairs.1 = (f32[768,128]{1,0:T(8,128)S(1)}, f32[768,1152]{1,0:T(8,128)S(1)}) custom-call(s32[1]{0:T(128)} %bitcast.odd.refs_0_, f32[1]{0:T(128)S(6)} %copy.21.log_scale.refs_1_, f32[1]{0:T(128)S(6)} %copy.22.logit_bias.refs_2_, bf16[768,1152]{1,0:T(8,128)(2,1)S(1)} %collective-permute-done.3.refs_3_, ...), custom_call_target="tpu_custom_call", output_to_operand_aliasing={{0}: (6, {})} | custom-call | flops 1 | bytes 1 | tf_op jit(solution)/shard_map/near_pairs/pallas_call | solution.py:326
  43.1 0.0 collective-permute-done.7.refs_6_
  43.1 0.0 collective-permute-done.6.refs_5_
  43.1 0.0 collective-permute-done.5.refs_4_
  43.1 0.0 collective-permute-done.4.refs_3_
  43.1 6.6 %add_pairs.3 = (f32[2,768,1152]{2,1,0:T(8,128)S(1)}, f32[768,128]{1,0:T(8,128)S(1)}, bf16[768,1152]{1,0:T(8,128)(2,1)S(1)}, f32[768,1152]{1,0:T(8,128)}, f32[768,1152]{1,0:T(8,128)}) custom-call(s32[1]{0:T(128)} %bitcast.odd.refs_0_, f32[1]{0:T(128)S(6)} %copy.21.log_scale.refs_1_, ...), custom_call_target="tpu_custom_call", output_to_operand_aliasing={{0}: (8, {}), {1}: (9, {})} | custom-call | flops 1 | bytes 1 | tf_op jit(solution)/shard_map/add_pairs/pallas_call | solution.py:295
  49.7 0.0 collective-permute-done.2.refs_3_
  49.7 5.2 %far_pairs.1 = (f32[768]{0:T(1024)}, f32[768,1152]{1,0:T(8,128)}, f32[768,1152]{1,0:T(8,128)}) custom-call(s32[1]{0:T(128)} %bitcast.odd.refs_0_, f32[1]{0:T(128)S(6)} %copy.21.log_scale.refs_1_, f32[1]{0:T(128)S(6)} %copy.22.logit_bias.refs_2_, bf16[368,1152]{1,0:T(8,128)(2,1)S(1)} %collective-permute-done.2.refs_3_, ...), custom_call_target="tpu_custom_call", output_to_operand_aliasing={{1}: (8, {}), {2}: (9, {})} | custom-call | flops 1 | bytes 1 | tf_op jit(solution)/shard_map/far_pairs/pallas_call | solution.py:343
Async XLA Ops:
  2.1 31.0 %collective-permute-start.3 = (bf16[768,1152]{1,0:T(8,128)(2,1)S(1)}, bf16[768,1152]{1,0:T(8,128)(2,1)S(1)}, u32[]{:S(2)}, u32[]{:S(2)}) collective-permute-start(bf16[768,1152]{1,0:T(8,128)(2,1)S(1)} %pick.1.far), channel_id=1, source_target_pairs={{0,254},{1,3},{2,0},{3,5},{4,2},{5,7},{6,4},{7,9},{8,6},{9,11},{10... | collective-permute-start | bytes 5308424 | tf_op jit(solution)/shard_map/ppermute | solution.py:371
  6.3 13.4 %collective-permute-start = (bf16[400,1152]{1,0:T(8,128)(2,1)S(1)}, bf16[400,1152]{1,0:T(8,128)(2,1)S(1)}, u32[]{:S(2)}, u32[]{:S(2)}) collective-permute-start(bf16[400,1152]{1,0:T(8,128)(2,1)S(1)} %get-tuple-element.25), channel_id=1, source_target_pairs={{0,1},{1,0},{2,3},{3,2},{4,5},{5,4},{6,7},{7,6},{8,9},{9,8},{10,11... | collective-permute-start | bytes 2764808 | tf_op jit(solution)/shard_map/ppermute | solution.py:371
  16.3 3.3 %collective-permute-start.1 = (bf16[368,1152]{1,0:T(8,128)(2,1)S(1)}, bf16[368,1152]{1,0:T(8,128)(2,1)S(1)}, u32[]{:S(2)}, u32[]{:S(2)}) collective-permute-start(bf16[368,1152]{1,0:T(8,128)(2,1)S(1)} %get-tuple-element.26), channel_id=1, source_target_pairs={{0,1},{1,0},{2,3},{3,2},{4,5},{5,4},{6,7},{7,6},{8,9},{9,8},{10,11... | collective-permute-start | bytes 2543624 | tf_op jit(solution)/shard_map/ppermute | solution.py:371
  19.6 23.5 %collective-permute-start.7 = (bf16[400,1152]{1,0:T(8,128)(2,1)S(1)}, bf16[400,1152]{1,0:T(8,128)(2,1)S(1)}, u32[]{:S(2)}, u32[]{:S(2)}) collective-permute-start(bf16[400,1152]{1,0:T(8,128)(2,1)S(1)} %collective-permute-done.refs_3_), channel_id=1, source_target_pairs={{0,255},{1,2},{2,1},{3,4},{4,3},{5,6},{6,5},{7,8},{8,7},{9,10},{10... | collective-permute-start | bytes 2764808 | tf_op jit(solution)/shard_map/ppermute | solution.py:371
  25.2 24.5 %collective-permute-start.2 = (bf16[368,1152]{1,0:T(8,128)(2,1)S(1)}, bf16[368,1152]{1,0:T(8,128)(2,1)S(1)}, u32[]{:S(2)}, u32[]{:S(2)}) collective-permute-start(bf16[368,1152]{1,0:T(8,128)(2,1)S(1)} %collective-permute-done.1.refs_4_), channel_id=1, source_target_pairs={{0,255},{1,2},{2,1},{3,4},{4,3},{5,6},{6,5},{7,8},{8,7},{9,10},{10... | collective-permute-start | bytes 2543624 | tf_op jit(solution)/shard_map/ppermute | solution.py:371
  33.3 9.8 %collective-permute-start.6 = (bf16[256,1152]{1,0:T(8,128)(2,1)S(1)}, bf16[256,1152]{1,0:T(8,128)(2,1)S(1)}, u32[]{:S(2)}, u32[]{:S(2)}) collective-permute-start(bf16[256,1152]{1,0:T(8,128)(2,1)S(1)} %get-tuple-element.47), channel_id=1, source_target_pairs={{0,1},{1,0},{2,3},{3,2},{4,5},{5,4},{6,7},{7,6},{8,9},{9,8},{10,11... | collective-permute-start | bytes 1769480 | tf_op jit(solution)/shard_map/ppermute | solution.py:371
  37.5 5.6 %collective-permute-start.5 = (bf16[256,1152]{1,0:T(8,128)(2,1)S(1)}, bf16[256,1152]{1,0:T(8,128)(2,1)S(1)}, u32[]{:S(2)}, u32[]{:S(2)}) collective-permute-start(bf16[256,1152]{1,0:T(8,128)(2,1)S(1)} %get-tuple-element.48), channel_id=1, source_target_pairs={{0,1},{1,0},{2,3},{3,2},{4,5},{5,4},{6,7},{7,6},{8,9},{9,8},{10,11... | collective-permute-start | bytes 1769480 | tf_op jit(solution)/shard_map/ppermute | solution.py:371
  37.6 5.5 %collective-permute-start.4 = (bf16[256,1152]{1,0:T(8,128)(2,1)S(1)}, bf16[256,1152]{1,0:T(8,128)(2,1)S(1)}, u32[]{:S(2)}, u32[]{:S(2)}) collective-permute-start(bf16[256,1152]{1,0:T(8,128)(2,1)S(1)} %get-tuple-element.49), channel_id=1, source_target_pairs={{0,1},{1,0},{2,3},{3,2},{4,5},{5,4},{6,7},{7,6},{8,9},{9,8},{10,11... | collective-permute-start | bytes 1769480 | tf_op jit(solution)/shard_map/ppermute | solution.py:371

commit v7 on v6

--- a/solution.py
+++ b/solution.py
@@ -73,10 +73,21 @@
         pltpu.make_async_copy(source, target, sem).start()
 
 
-def pick_kernel(odd, images, texts, far, sem):
-    copy_if(odd[0] == 1, texts, far, sem)
-    copy_if(odd[0] == 0, images, far, sem)
-    pltpu.make_async_copy(images, far, sem).wait()
+def pick_kernel(odd, images, texts, far, sems):
+    pieces = [pl.ds(start, LANES) for start in range(0, RB, LANES)]
+
+    @pl.when(odd[0] == 1)
+    def _():
+        for at, here in enumerate(pieces):
+            pltpu.make_async_copy(texts.at[here], far.at[here], sems.at[at]).start()
+
+    @pl.when(odd[0] == 0)
+    def _():
+        for at, here in enumerate(pieces):
+            pltpu.make_async_copy(images.at[here], far.at[here], sems.at[at]).start()
+
+    for at, here in enumerate(pieces):
+        pltpu.make_async_copy(images.at[here], far.at[here], sems.at[at]).wait()
 
 
 def pick(odd, images, texts):
@@ -85,7 +96,7 @@
         in_specs=[SCALARS, ANYWHERE, ANYWHERE],
         out_specs=RESIDENT,
         out_shape=pltpu.VMEM((RB, D), jnp.bfloat16),
-        scratch_shapes=[pltpu.SemaphoreType.DMA],
+        scratch_shapes=[pltpu.SemaphoreType.DMA((RB // LANES,))],
         cost_estimate=NO_COST,
         name="pick",
     )(odd, in_hbm(images), in_hbm(texts))

time: 55.5 us -> 55.4 us (level)
  no operation moved by 1% of the time
where the time goes in v7:
time: 55.4 us; the launch traced here: 55 us
  Pallas kernels  30 us (54%)
  starting transfers between devices  19 us (34%)
  waiting for transfers between devices  3.67 us (7%)
  between operations  2.19 us (4%)
    ppermute x8, starting transfers between devices, send(): return lax.ppermute(block, 'blk', pairs)  19 us
    pallas_call x2, Pallas kernels, add_pairs(): pl.pallas_call(functools.partial(add_kernel, side=side, pieces=len(others...  10.8 us
    pallas_call x1, Pallas kernels, own_pairs(): pl.pallas_call(own_kernel, in_specs=[SCALARS] * 3 + [RESIDENT], out_specs...  5.59 us
    pallas_call x1, Pallas kernels, far_pairs(): pl.pallas_call(far_kernel, in_specs=[SCALARS] * 3 + [RESIDENT] * 5 + [ANY...  5.16 us
    pallas_call x1, Pallas kernels, near_pairs(): pl.pallas_call(near_kernel, in_specs=[SCALARS] * 3 + [RESIDENT] * 5, out_...  5.08 us
    ppermute x8, waiting for transfers between devices, send(): return lax.ppermute(block, 'blk', pairs)  3.67 us
    pallas_call x1, Pallas kernels, prepare(): pl.pallas_call(prepare_kernel, in_specs=[SCALARS, ANYWHERE, ANYWHERE, RES...  2 us
    pallas_call x1, Pallas kernels, pick(): pl.pallas_call(pick_kernel, in_specs=[SCALARS, ANYWHERE, ANYWHERE], out_s...  1.46 us
  transfers between devices with their start and end apart: 8, of which 2 were waited for; matrix products, arithmetic and copies ran while one was open for 0% of the time, Pallas kernels for 43%

profile of v7, /device:TPU:1, one launch (start us, length us, event | category | flops | bytes accessed | tf_op | source)
XLA Modules:
  0.0 55.0 jit_solution(18149509513332493543)
XLA Ops:
  0.6 1.5 %pick.1.far = bf16[768,1152]{1,0:T(8,128)(2,1)S(1)} custom-call(s32[1]{0:T(128)} %bitcast.odd.refs_0_, bf16[768,1152]{1,0:T(8,128)(2,1)} %refs_10_.1, bf16[768,1152]{1,0:T(8,128)(2,1)} %refs_11_.1), custom_call_target="tpu_custom_call" | custom-call | flops 1 | bytes 1 | tf_op jit(solution)/shard_map/pick/pallas_call | solution.py:94
  2.1 2.1 %collective-permute-start.3 = (bf16[768,1152]{1,0:T(8,128)(2,1)S(1)}, bf16[768,1152]{1,0:T(8,128)(2,1)S(1)}, u32[]{:S(2)}, u32[]{:S(2)}) collective-permute-start(bf16[768,1152]{1,0:T(8,128)(2,1)S(1)} %pick.1.far), channel_id=1, source_target_pairs={{0,254},{1,3},{2,0},{3,5},{4,2},{5,7},{6,4},{7,9},{8,6},{9,11},{10... | collective-permute-start | bytes 5308424 | tf_op jit(solution)/shard_map/ppermute | solution.py:382
  4.2 2.0 %prepare.1 = (bf16[2,768,1152]{2,1,0:T(8,128)(2,1)S(1)}, bf16[400,1152]{1,0:T(8,128)(2,1)S(1)}, bf16[368,1152]{1,0:T(8,128)(2,1)S(1)}) custom-call(s32[1]{0:T(128)} %bitcast.odd.refs_0_, bf16[768,1152]{1,0:T(8,128)(2,1)} %refs_10_.1, bf16[768,1152]{1,0:T(8,128)(2,1)} %refs_11_.1, bf16[768,1152]{1,0:T(8,128)(2,1)S(1)} %pick.1.far), custom_call_target="tpu_custom_call" | custom-call | flops 1 | bytes 1 | tf_op jit(solution)/shard_map/prepare/pallas_call | solution.py:124
  6.2 10.1 %collective-permute-start = (bf16[400,1152]{1,0:T(8,128)(2,1)S(1)}, bf16[400,1152]{1,0:T(8,128)(2,1)S(1)}, u32[]{:S(2)}, u32[]{:S(2)}) collective-permute-start(bf16[400,1152]{1,0:T(8,128)(2,1)S(1)} %get-tuple-element.25), channel_id=1, source_target_pairs={{0,1},{1,0},{2,3},{3,2},{4,5},{5,4},{6,7},{7,6},{8,9},{9,8},{10,11... | collective-permute-start | bytes 2764808 | tf_op jit(solution)/shard_map/ppermute | solution.py:382
  16.3 0.1 collective-permute-start.1
  17.7 1.9 %collective-permute-done.1.refs_4_ = bf16[368,1152]{1,0:T(8,128)(2,1)S(1)} collective-permute-done((bf16[368,1152]{1,0:T(8,128)(2,1)S(1)}, bf16[368,1152]{1,0:T(8,128)(2,1)S(1)}, u32[]{:S(2)}, u32[]{:S(2)}) %collective-permute-start.1) | collective-permute-done | bytes 847904 | tf_op jit(solution)/shard_map/ppermute | solution.py:382
  19.6 0.0 collective-permute-done.refs_3_
  19.6 0.0 collective-permute-start.7
  19.6 5.6 %own_pairs.1 = (f32[2,768,1152]{2,1,0:T(8,128)S(1)}, f32[768,128]{1,0:T(8,128)S(1)}) custom-call(s32[1]{0:T(128)} %bitcast.odd.refs_0_, f32[1]{0:T(128)S(6)} %copy.21.log_scale.refs_1_, f32[1]{0:T(128)S(6)} %copy.22.logit_bias.refs_2_, bf16[2,768,1152]{2,1,0:T(8,128)(2,1)S(1)} %get-tuple-element.29.emb.refs_5_.refs_4_.refs_7_), custom_call_target="tpu_custom_call" | custom-call | flops 1 | bytes 1 | tf_op jit(solution)/shard_map/own_pairs/pallas_call | solution.py:169
  25.2 2.0 %collective-permute-start.2 = (bf16[368,1152]{1,0:T(8,128)(2,1)S(1)}, bf16[368,1152]{1,0:T(8,128)(2,1)S(1)}, u32[]{:S(2)}, u32[]{:S(2)}) collective-permute-start(bf16[368,1152]{1,0:T(8,128)(2,1)S(1)} %collective-permute-done.1.refs_4_), channel_id=1, source_target_pairs={{0,255},{1,2},{2,1},{3,4},{4,3},{5,6},{6,5},{7,8},{8,7},{9,10},{10... | collective-permute-start | bytes 2543624 | tf_op jit(solution)/shard_map/ppermute | solution.py:382
  27.2 4.2 %add_pairs.2 = (f32[2,768,1152]{2,1,0:T(8,128)S(1)}, f32[768,128]{1,0:T(8,128)S(1)}, bf16[768,1152]{1,0:T(8,128)(2,1)S(1)}) custom-call(s32[1]{0:T(128)} %bitcast.odd.refs_0_, f32[1]{0:T(128)S(6)} %copy.21.log_scale.refs_1_, f32[1]{0:T(128)S(6)} %copy.22.logit_bias.refs_2_, ...), custom_call_target="tpu_custom_call", output_to_operand_aliasing={{0}: (6, {}), {1}: (7, {})} | custom-call | flops 1 | bytes 1 | tf_op jit(solution)/shard_map/add_pairs/pallas_call | solution.py:306
  31.4 1.7 %collective-permute-done.3.refs_3_ = bf16[768,1152]{1,0:T(8,128)(2,1)S(1)} collective-permute-done((bf16[768,1152]{1,0:T(8,128)(2,1)S(1)}, bf16[768,1152]{1,0:T(8,128)(2,1)S(1)}, u32[]{:S(2)}, u32[]{:S(2)}) %collective-permute-start.3) | collective-permute-done | bytes 1769504 | tf_op jit(solution)/shard_map/ppermute | solution.py:382
  33.2 0.1 fusion
  33.3 4.2 %collective-permute-start.6 = (bf16[256,1152]{1,0:T(8,128)(2,1)S(1)}, bf16[256,1152]{1,0:T(8,128)(2,1)S(1)}, u32[]{:S(2)}, u32[]{:S(2)}) collective-permute-start(bf16[256,1152]{1,0:T(8,128)(2,1)S(1)} %get-tuple-element.47), channel_id=1, source_target_pairs={{0,1},{1,0},{2,3},{3,2},{4,5},{5,4},{6,7},{7,6},{8,9},{9,8},{10,11... | collective-permute-start | bytes 1769480 | tf_op jit(solution)/shard_map/ppermute | solution.py:382
  37.5 0.1 collective-permute-start.5
  37.6 0.4 collective-permute-start.4
  38.0 5.1 %near_pairs.1 = (f32[768,128]{1,0:T(8,128)S(1)}, f32[768,1152]{1,0:T(8,128)S(1)}) custom-call(s32[1]{0:T(128)} %bitcast.odd.refs_0_, f32[1]{0:T(128)S(6)} %copy.21.log_scale.refs_1_, f32[1]{0:T(128)S(6)} %copy.22.logit_bias.refs_2_, bf16[768,1152]{1,0:T(8,128)(2,1)S(1)} %collective-permute-done.3.refs_3_, ...), custom_call_target="tpu_custom_call", output_to_operand_aliasing={{0}: (6, {})} | custom-call | flops 1 | bytes 1 | tf_op jit(solution)/shard_map/near_pairs/pallas_call | solution.py:337
  43.1 0.0 collective-permute-done.7.refs_6_
  43.1 0.0 collective-permute-done.6.refs_5_
  43.1 0.0 collective-permute-done.5.refs_4_
  43.1 0.0 collective-permute-done.4.refs_3_
  43.1 6.6 %add_pairs.3 = (f32[2,768,1152]{2,1,0:T(8,128)S(1)}, f32[768,128]{1,0:T(8,128)S(1)}, bf16[768,1152]{1,0:T(8,128)(2,1)S(1)}, f32[768,1152]{1,0:T(8,128)}, f32[768,1152]{1,0:T(8,128)}) custom-call(s32[1]{0:T(128)} %bitcast.odd.refs_0_, f32[1]{0:T(128)S(6)} %copy.21.log_scale.refs_1_, ...), custom_call_target="tpu_custom_call", output_to_operand_aliasing={{0}: (8, {}), {1}: (9, {})} | custom-call | flops 1 | bytes 1 | tf_op jit(solution)/shard_map/add_pairs/pallas_call | solution.py:306
  49.7 0.0 collective-permute-done.2.refs_3_
  49.7 5.2 %far_pairs.1 = (f32[768]{0:T(1024)}, f32[768,1152]{1,0:T(8,128)}, f32[768,1152]{1,0:T(8,128)}) custom-call(s32[1]{0:T(128)} %bitcast.odd.refs_0_, f32[1]{0:T(128)S(6)} %copy.21.log_scale.refs_1_, f32[1]{0:T(128)S(6)} %copy.22.logit_bias.refs_2_, bf16[368,1152]{1,0:T(8,128)(2,1)S(1)} %collective-permute-done.2.refs_3_, ...), custom_call_target="tpu_custom_call", output_to_operand_aliasing={{1}: (8, {}), {2}: (9, {})} | custom-call | flops 1 | bytes 1 | tf_op jit(solution)/shard_map/far_pairs/pallas_call | solution.py:354
Async XLA Ops:
  2.1 31.0 %collective-permute-start.3 = (bf16[768,1152]{1,0:T(8,128)(2,1)S(1)}, bf16[768,1152]{1,0:T(8,128)(2,1)S(1)}, u32[]{:S(2)}, u32[]{:S(2)}) collective-permute-start(bf16[768,1152]{1,0:T(8,128)(2,1)S(1)} %pick.1.far), channel_id=1, source_target_pairs={{0,254},{1,3},{2,0},{3,5},{4,2},{5,7},{6,4},{7,9},{8,6},{9,11},{10... | collective-permute-start | bytes 5308424 | tf_op jit(solution)/shard_map/ppermute | solution.py:382
  6.2 13.4 %collective-permute-start = (bf16[400,1152]{1,0:T(8,128)(2,1)S(1)}, bf16[400,1152]{1,0:T(8,128)(2,1)S(1)}, u32[]{:S(2)}, u32[]{:S(2)}) collective-permute-start(bf16[400,1152]{1,0:T(8,128)(2,1)S(1)} %get-tuple-element.25), channel_id=1, source_target_pairs={{0,1},{1,0},{2,3},{3,2},{4,5},{5,4},{6,7},{7,6},{8,9},{9,8},{10,11... | collective-permute-start | bytes 2764808 | tf_op jit(solution)/shard_map/ppermute | solution.py:382
  16.3 3.3 %collective-permute-start.1 = (bf16[368,1152]{1,0:T(8,128)(2,1)S(1)}, bf16[368,1152]{1,0:T(8,128)(2,1)S(1)}, u32[]{:S(2)}, u32[]{:S(2)}) collective-permute-start(bf16[368,1152]{1,0:T(8,128)(2,1)S(1)} %get-tuple-element.26), channel_id=1, source_target_pairs={{0,1},{1,0},{2,3},{3,2},{4,5},{5,4},{6,7},{7,6},{8,9},{9,8},{10,11... | collective-permute-start | bytes 2543624 | tf_op jit(solution)/shard_map/ppermute | solution.py:382
  19.6 23.4 %collective-permute-start.7 = (bf16[400,1152]{1,0:T(8,128)(2,1)S(1)}, bf16[400,1152]{1,0:T(8,128)(2,1)S(1)}, u32[]{:S(2)}, u32[]{:S(2)}) collective-permute-start(bf16[400,1152]{1,0:T(8,128)(2,1)S(1)} %collective-permute-done.refs_3_), channel_id=1, source_target_pairs={{0,255},{1,2},{2,1},{3,4},{4,3},{5,6},{6,5},{7,8},{8,7},{9,10},{10... | collective-permute-start | bytes 2764808 | tf_op jit(solution)/shard_map/ppermute | solution.py:382
  25.2 24.5 %collective-permute-start.2 = (bf16[368,1152]{1,0:T(8,128)(2,1)S(1)}, bf16[368,1152]{1,0:T(8,128)(2,1)S(1)}, u32[]{:S(2)}, u32[]{:S(2)}) collective-permute-start(bf16[368,1152]{1,0:T(8,128)(2,1)S(1)} %collective-permute-done.1.refs_4_), channel_id=1, source_target_pairs={{0,255},{1,2},{2,1},{3,4},{4,3},{5,6},{6,5},{7,8},{8,7},{9,10},{10... | collective-permute-start | bytes 2543624 | tf_op jit(solution)/shard_map/ppermute | solution.py:382
  33.3 9.8 %collective-permute-start.6 = (bf16[256,1152]{1,0:T(8,128)(2,1)S(1)}, bf16[256,1152]{1,0:T(8,128)(2,1)S(1)}, u32[]{:S(2)}, u32[]{:S(2)}) collective-permute-start(bf16[256,1152]{1,0:T(8,128)(2,1)S(1)} %get-tuple-element.47), channel_id=1, source_target_pairs={{0,1},{1,0},{2,3},{3,2},{4,5},{5,4},{6,7},{7,6},{8,9},{9,8},{10,11... | collective-permute-start | bytes 1769480 | tf_op jit(solution)/shard_map/ppermute | solution.py:382
  37.5 5.6 %collective-permute-start.5 = (bf16[256,1152]{1,0:T(8,128)(2,1)S(1)}, bf16[256,1152]{1,0:T(8,128)(2,1)S(1)}, u32[]{:S(2)}, u32[]{:S(2)}) collective-permute-start(bf16[256,1152]{1,0:T(8,128)(2,1)S(1)} %get-tuple-element.48), channel_id=1, source_target_pairs={{0,1},{1,0},{2,3},{3,2},{4,5},{5,4},{6,7},{7,6},{8,9},{9,8},{10,11... | collective-permute-start | bytes 1769480 | tf_op jit(solution)/shard_map/ppermute | solution.py:382
  37.6 5.5 %collective-permute-start.4 = (bf16[256,1152]{1,0:T(8,128)(2,1)S(1)}, bf16[256,1152]{1,0:T(8,128)(2,1)S(1)}, u32[]{:S(2)}, u32[]{:S(2)}) collective-permute-start(bf16[256,1152]{1,0:T(8,128)(2,1)S(1)} %get-tuple-element.49), channel_id=1, source_target_pairs={{0,1},{1,0},{2,3},{3,2},{4,5},{5,4},{6,7},{7,6},{8,9},{9,8},{10,11... | collective-permute-start | bytes 1769480 | tf_op jit(solution)/shard_map/ppermute | solution.py:382
